TPU v7x, 32 devices: a whole 2x2x4 slice. The times are simulated.
32 devices in a mesh: dp: 16 (over z, y, x), fsdp: 2 (over core).
Axes of the slice: x: 2, y: 2, z: 4, core: 2. Of those that a mesh axis runs over, the one named last changes fastest.
Arguments:
- tokens: bfloat16 [32768, 1024], P(('dp', 'fsdp')), may hold values from -6 to 6
- cotangent: bfloat16 [32768, 1024], P(('dp', 'fsdp')), may hold values from -6 to 6
- lengths: int32 [2], replicated, may hold values from 2048 to 16384, as said below
- norm_gain: bfloat16 [1024], P(('dp', 'fsdp')), may hold values from 0.5 to 1.5
- norm_bias: bfloat16 [1024], P(('dp', 'fsdp')), may hold values from -1.25 to 1.25
- w_one: bfloat16 [1024, 3072], P(('dp', 'fsdp')), may hold values from -0.1875 to 0.1875
- b_one: bfloat16 [3072], P(('dp', 'fsdp')), may hold values from -1.25 to 1.25
- w_two: bfloat16 [1024, 512], P(('dp', 'fsdp')), may hold values from -0.1875 to 0.1875
- b_two: bfloat16 [512], P(('dp', 'fsdp')), may hold values from -1.25 to 1.25
- w_three: bfloat16 [512, 3072], P(('dp', 'fsdp')), may hold values from -0.25 to 0.25
- b_three: bfloat16 [3072], P(('dp', 'fsdp')), may hold values from -1.25 to 1.25
- w_four: bfloat16 [3072, 1024], P(('dp', 'fsdp')), may hold values from -0.109375 to 0.109375
- b_four: bfloat16 [1024], P(('dp', 'fsdp')), may hold values from -1.25 to 1.25
- log_rate: float32 [512, 512], P(('dp', 'fsdp')), may hold values from -9 to -3
- ssm_coeff: float32 [512, 512], P(('dp', 'fsdp')), may hold values from -0.009765625 to 0.009765625
- ssm_skip: float32 [512], P(('dp', 'fsdp')), may hold values from 0.5 to 1.5
Outputs:
- mixed: bfloat16 [32768, 1024], P(('dp', 'fsdp'))
- input_grad: bfloat16 [32768, 1024], P(('dp', 'fsdp'))
- grad_norm_gain: float32 [1024], P(('dp', 'fsdp'))
- grad_norm_bias: float32 [1024], P(('dp', 'fsdp'))
- grad_w_one: float32 [1024, 3072], P(('dp', 'fsdp'))
- grad_b_one: float32 [3072], P(('dp', 'fsdp'))
- grad_w_two: float32 [1024, 512], P(('dp', 'fsdp'))
- grad_b_two: float32 [512], P(('dp', 'fsdp'))
- grad_w_three: float32 [512, 3072], P(('dp', 'fsdp'))
- grad_b_three: float32 [3072], P(('dp', 'fsdp'))
- grad_w_four: float32 [3072, 1024], P(('dp', 'fsdp'))
- grad_b_four: float32 [1024], P(('dp', 'fsdp'))
- grad_log_rate: float32 [512, 512], P(('dp', 'fsdp'))
- grad_ssm_coeff: float32 [512, 512], P(('dp', 'fsdp'))
- grad_ssm_skip: float32 [512], P(('dp', 'fsdp'))
Inputs may be any that keep to these rules, and one draw needn't show every extreme that they name: `lengths`: every bucket's length is at least 2048; one bucket in every draw holds a full sequence of 16384 tokens.
All inputs are finite; a program needn't handle non-finite values.
Results may differ from a plain program's by a relative error of at most 0.0071.
Values may be sent and summed in bfloat16 or wider, within the bound.
No kernel may reach another device: no remote copies, remote signals or barrier semaphores. Data moves between devices by JAX's collectives and lax.ppermute only.
A program may use at most 192 MiB of HBM per device.

v0:
```python
import jax
import jax.numpy as jnp
from jax import lax
from jax.sharding import PartitionSpec as P

SEQ = 16384
QBLK = 256


HIGHEST = lax.Precision.HIGHEST
THREE_PASS = lax.Precision.HIGH


def state_mix(values, log_rate, ssm_coeff, ssm_skip, seq_len, block_len):
    chans, total = values.shape
    nstates = log_rate.shape[1]
    buckets = total // seq_len
    per_seq = seq_len // block_len
    all_blocks = total // block_len
    decay_rate = jnp.exp(log_rate)
    offsets = jnp.arange(block_len, dtype=jnp.int32)
    offsets_f = offsets.astype(jnp.float32)
    decay = jnp.exp(-decay_rate[:, :, None] * offsets_f[None, None, :])
    growth = jnp.exp(decay_rate[:, :, None] * offsets_f[None, None, :])
    weighted = ssm_coeff[:, :, None] * decay
    full_mat = jnp.einsum("hnt,hns->hts", weighted, growth, precision=HIGHEST)
    lower = offsets[:, None] >= offsets[None, :]
    toeplitz = jnp.where(lower[None], full_mat, 0.0)
    blocks = values.reshape(chans, all_blocks, block_len)
    inner_part = jnp.einsum("hts,hks->hkt", toeplitz, blocks, precision=THREE_PASS)
    block_ends = jnp.einsum("hks,hns->hkn", blocks, decay[:, :, ::-1], precision=THREE_PASS)
    block_ends = jnp.moveaxis(block_ends.reshape(chans, buckets, per_seq, nstates), 2, 0)
    carry_decay = jnp.exp(-decay_rate * block_len)[:, None, :]

    def advance(state_in, contrib):
        return (state_in * carry_decay + contrib, state_in)

    start = jnp.zeros((chans, buckets, nstates), jnp.float32)
    final_state, entering = lax.scan(advance, start, block_ends)
    entering = jnp.moveaxis(entering, 0, 2).reshape(chans, all_blocks, nstates)
    reach = weighted * jnp.exp(-decay_rate)[:, :, None]
    outer_part = jnp.einsum("hkn,hnt->hkt", entering, reach, precision=THREE_PASS)
    mixed_out = (inner_part + outer_part).reshape(chans, total)
    return mixed_out + ssm_skip[:, None] * values


def contract(left, right, left_dim, right_dim):
    return lax.dot_general(
        left, right, (((left_dim,), (right_dim,)), ((), ())), preferred_element_type=jnp.float32
    )


def gelu_slope(hidden):
    return (
        0.5 * (1.0 + lax.erf(hidden * 0.7071067811865476))
        + hidden * jnp.exp(-0.5 * hidden * hidden) * 0.3989422804014327
    )


def norm_parts(inputs):
    center = jnp.mean(inputs, axis=-1, keepdims=True)
    centered = inputs - center
    spread = jnp.mean(centered * centered, axis=-1, keepdims=True)
    inv_std = lax.rsqrt(spread + 1e-05)
    return (centered * inv_std, inv_std)


def norm_back(normed_grad, normal_hat, inv_std, gain_f):
    hat_grad = normed_grad * gain_f
    return inv_std * (
        hat_grad
        - jnp.mean(hat_grad, axis=-1, keepdims=True)
        - normal_hat * jnp.mean(hat_grad * normal_hat, axis=-1, keepdims=True)
    )


def per_device(
    tokens,
    cotangent,
    lengths,
    norm_gain,
    norm_bias,
    w_one,
    b_one,
    w_two,
    b_two,
    w_three,
    b_three,
    w_four,
    b_four,
    log_rate,
    ssm_coeff,
    ssm_skip,
):
    tok_dev = tokens.shape[0]
    (
        gain_full,
        nbias_full,
        wone_full,
        bone_full,
        wtwo_full,
        btwo_full,
        wthree_full,
        bthree_full,
        wfour_full,
        bfour_full,
    ) = (
        lax.all_gather(norm_gain, ("dp", "fsdp"), axis=0, tiled=True),
        lax.all_gather(norm_bias, ("dp", "fsdp"), axis=0, tiled=True),
        lax.all_gather(w_one, ("dp", "fsdp"), axis=0, tiled=True),
        lax.all_gather(b_one, ("dp", "fsdp"), axis=0, tiled=True),
        lax.all_gather(w_two, ("dp", "fsdp"), axis=0, tiled=True),
        lax.all_gather(b_two, ("dp", "fsdp"), axis=0, tiled=True),
        lax.all_gather(w_three, ("dp", "fsdp"), axis=0, tiled=True),
        lax.all_gather(b_three, ("dp", "fsdp"), axis=0, tiled=True),
        lax.all_gather(w_four, ("dp", "fsdp"), axis=0, tiled=True),
        lax.all_gather(b_four, ("dp", "fsdp"), axis=0, tiled=True),
    )
    gain_f = gain_full.astype(jnp.float32)
    nbias_f = nbias_full.astype(jnp.float32)
    count = lengths.shape[0]
    bucket_range = jnp.arange(count, dtype=jnp.int32)
    place = lax.axis_index(("dp", "fsdp")) * tok_dev + jnp.arange(tok_dev, dtype=jnp.int32)
    limit = jnp.sum(
        jnp.where((place // SEQ)[:, None] == bucket_range[None, :], lengths[None, :], 0), axis=1
    )
    live = (place % SEQ < limit).astype(jnp.float32)[:, None]

    def local_mix(values, rates, coeffs, skips):
        return state_mix(values, rates, coeffs, skips, SEQ, QBLK)

    inputs = tokens.astype(jnp.float32)
    normal_hat, inv_std = norm_parts(inputs)
    normed_bf = (normal_hat * gain_f + nbias_f).astype(jnp.bfloat16)
    hidden_one = jnp.dot(
        normed_bf, wone_full, preferred_element_type=jnp.float32
    ) + bone_full.astype(jnp.float32)
    act_one = jax.nn.gelu(hidden_one, approximate=False)
    hidden_two_t = contract(wtwo_full, normed_bf, 0, 1) + btwo_full.astype(jnp.float32)[:, None]
    reduced_t = jax.nn.gelu(hidden_two_t, approximate=False).astype(jnp.bfloat16)
    reduced_ch = lax.all_to_all(reduced_t, ("dp", "fsdp"), split_axis=0, concat_axis=1, tiled=True)
    mixer_ch, mixer_pull = jax.vjp(
        local_mix, reduced_ch.astype(jnp.float32), log_rate, ssm_coeff, ssm_skip
    )
    mixer_t = lax.all_to_all(
        mixer_ch.astype(jnp.bfloat16), ("dp", "fsdp"), split_axis=1, concat_axis=0, tiled=True
    )
    gate = contract(mixer_t, wthree_full, 0, 0) + bthree_full.astype(jnp.float32)
    product_bf = (act_one * gate).astype(jnp.bfloat16)
    branch = jnp.dot(
        product_bf, wfour_full, preferred_element_type=jnp.float32
    ) + bfour_full.astype(jnp.float32)
    mixed = (live * (inputs + branch)).astype(jnp.bfloat16)
    out_grad = (live * cotangent.astype(jnp.float32)).astype(jnp.bfloat16)
    grad_wfour = contract(product_bf, out_grad, 0, 0)
    grad_bfour = jnp.sum(out_grad.astype(jnp.float32), axis=0)
    prod_grad = contract(out_grad, wfour_full, 1, 1)
    act_grad = prod_grad * gate
    gate_grad = (prod_grad * act_one).astype(jnp.bfloat16)
    grad_wthree = contract(mixer_t, gate_grad, 1, 0)
    grad_bthree = jnp.sum(gate_grad.astype(jnp.float32), axis=0)
    mixer_grad_t = contract(wthree_full, gate_grad, 1, 1).astype(jnp.bfloat16)
    mixer_grad_ch = lax.all_to_all(
        mixer_grad_t, ("dp", "fsdp"), split_axis=0, concat_axis=1, tiled=True
    )
    reduced_grad_ch, grad_rate, grad_coeff, grad_skip = mixer_pull(
        mixer_grad_ch.astype(jnp.float32)
    )
    reduced_grad_t = lax.all_to_all(
        reduced_grad_ch.astype(jnp.bfloat16),
        ("dp", "fsdp"),
        split_axis=1,
        concat_axis=0,
        tiled=True,
    )
    hidden_two_grad = (reduced_grad_t.astype(jnp.float32) * gelu_slope(hidden_two_t)).astype(
        jnp.bfloat16
    )
    hidden_one_grad = (act_grad * gelu_slope(hidden_one)).astype(jnp.bfloat16)
    grad_wone = contract(normed_bf, hidden_one_grad, 0, 0)
    grad_bone = jnp.sum(hidden_one_grad.astype(jnp.float32), axis=0)
    grad_wtwo = contract(normed_bf, hidden_two_grad, 0, 1)
    grad_btwo = jnp.sum(hidden_two_grad.astype(jnp.float32), axis=1)
    normed_grad = contract(hidden_one_grad, wone_full, 1, 1) + contract(
        hidden_two_grad, wtwo_full, 0, 1
    )
    grad_gain = jnp.sum(normed_grad * normal_hat, axis=0)
    grad_nbias = jnp.sum(normed_grad, axis=0)
    input_grad = (
        out_grad.astype(jnp.float32) + norm_back(normed_grad, normal_hat, inv_std, gain_f)
    ).astype(jnp.bfloat16)
    (
        sum_gain,
        sum_nbias,
        sum_one,
        sum_bone,
        sum_two,
        sum_btwo,
        sum_three,
        sum_bthree,
        sum_four,
        sum_bfour,
    ) = (
        lax.psum_scatter(grad_gain, ("dp", "fsdp"), scatter_dimension=0, tiled=True),
        lax.psum_scatter(grad_nbias, ("dp", "fsdp"), scatter_dimension=0, tiled=True),
        lax.psum_scatter(grad_wone, ("dp", "fsdp"), scatter_dimension=0, tiled=True),
        lax.psum_scatter(grad_bone, ("dp", "fsdp"), scatter_dimension=0, tiled=True),
        lax.psum_scatter(grad_wtwo, ("dp", "fsdp"), scatter_dimension=0, tiled=True),
        lax.psum_scatter(grad_btwo, ("dp", "fsdp"), scatter_dimension=0, tiled=True),
        lax.psum_scatter(grad_wthree, ("dp", "fsdp"), scatter_dimension=0, tiled=True),
        lax.psum_scatter(grad_bthree, ("dp", "fsdp"), scatter_dimension=0, tiled=True),
        lax.psum_scatter(grad_wfour, ("dp", "fsdp"), scatter_dimension=0, tiled=True),
        lax.psum_scatter(grad_bfour, ("dp", "fsdp"), scatter_dimension=0, tiled=True),
    )
    return (
        mixed,
        input_grad,
        sum_gain,
        sum_nbias,
        sum_one,
        sum_bone,
        sum_two,
        sum_btwo,
        sum_three,
        sum_bthree,
        sum_four,
        sum_bfour,
        grad_rate,
        grad_coeff,
        grad_skip,
    )


def solution(mesh):
    in_specs = (
        P(("dp", "fsdp"), None),
        P(("dp", "fsdp"), None),
        P(),
        P(("dp", "fsdp")),
        P(("dp", "fsdp")),
        P(("dp", "fsdp"), None),
        P(("dp", "fsdp")),
        P(("dp", "fsdp"), None),
        P(("dp", "fsdp")),
        P(("dp", "fsdp"), None),
        P(("dp", "fsdp")),
        P(("dp", "fsdp"), None),
        P(("dp", "fsdp")),
        P(("dp", "fsdp"), None),
        P(("dp", "fsdp"), None),
        P(("dp", "fsdp")),
    )
    out_specs = (
        P(("dp", "fsdp"), None),
        P(("dp", "fsdp"), None),
        P(("dp", "fsdp")),
        P(("dp", "fsdp")),
        P(("dp", "fsdp"), None),
        P(("dp", "fsdp")),
        P(("dp", "fsdp"), None),
        P(("dp", "fsdp")),
        P(("dp", "fsdp"), None),
        P(("dp", "fsdp")),
        P(("dp", "fsdp"), None),
        P(("dp", "fsdp")),
        P(("dp", "fsdp"), None),
        P(("dp", "fsdp"), None),
        P(("dp", "fsdp")),
    )
    return jax.shard_map(
        per_device, mesh=mesh, in_specs=in_specs, out_specs=out_specs, check_vma=False
    )
```

profile of v0, /device:TPU:0, one launch (start us, length us, event | category | flops | bytes accessed | tf_op | source)
XLA Modules:
  0.0 1296.1 jit_solution(9802818382675118142)
XLA Ops:
  14.5 42.3 %all-reduce.13 = (bf16[1024]{0:T(1024)(128)(2,1)}, bf16[1024]{0:T(1024)(128)(2,1)S(1)}, bf16[1024]{0:T(1024)(128)(2,1)S(1)}, bf16[3072]{0:T(1024)(128)(2,1)S(1)}...) all-reduce(bf16[1024]{0:T(1024)(128)(2,1)S(1)} %dynamic-update-slic, ...), channel_id=1, replica_groups=mesh['dp'=16,'fsdp'=2] {'dp','fsdp'}, use_global_device_ids=true, to_apply=%add.5 | all-reduce | flops 9728 | bytes 38912
  61.1 6.2 all-gather.7.cloned.1.call-done
  67.3 8.7 fusion.75
  76.0 3.7 all-to-all-start
  80.3 4.4 multiply_exponential_fusion.3
  84.8 64.4 %rev.6 = f32[16,512,256]{1,2,0:T(8,128)} reverse(f32[16,512,256]{1,2,0:T(8,128)} %multiply_exponential_fusion.3), dimensions={2} | reverse | bytes 16777216 | tf_op jit(solution)/shard_map/jvp()/rev | solution.py:31
  149.3 11.4 fusion.19
  165.0 5.7 fusion.146
  170.7 5.3 copy.145
  175.9 102.3 %while.32 = (s32[]{:T(128)}, f32[16,2,512]{2,1,0:T(2,128)S(1)}, f32[64,16,2,512]{3,2,1,0:T(2,128)}, f32[16,1,512]{2,0,1:T(8,128)S(1)}, f32[64,16,2,512]{3,2,1,0:T(2,128)}, /*index=5*/s32[]{:T(128)}, s32[]{:T(128)}) while((s32[]{:T(128)}, f32[16,2,512]{2,1,0:T(2,128)S(1)}, f32[64,16,2,512]{3,2,1,0:T(2,128)}, ...), condition=%wide.region_4.5_spmd.clone, body=%wide.region_3.4_spmd.clone.sunk | while | flops 65539 | bytes 360552 | solution.py:39
  278.2 4.8 copy.93
  285.1 6.4 fusion.108
  291.4 2.9 reshape.195
  294.3 3.8 fusion.69
  298.2 5.9 all-to-all-start.1
  304.3 26.0 %all-to-all-done.1 = bf16[16,32,1024]{2,0,1:T(8,128)(2,1)S(1)} async-done(((bf16[16,32,1024]{2,0,1:T(8,128)(2,1)}), bf16[16,32,1024]{2,0,1:T(8,128)(2,1)S(1)}, u32[]{:S(2)}, u32[]{:S(2)}) %all-to-all-start.1) | async-done | bytes 1048608 | tf_op jit(solution)/shard_map/all_to_all | solution.py:145
  330.3 8.6 fusion.147
  339.0 12.2 fusion.134
  351.1 46.4 %convert_reduce_fusion.1 = (f32[3072]{0:T(1024)}, bf16[1024,3072]{1,0:T(8,128)(2,1)}, f32[3072]{0:T(1024)}, bf16[1024,3072]{1,0:T(8,128)(2,1)S(1)}, f32[1024,3072]{1,0:T(8,128)}) fusion(f32[3072]{0:T(1024)S(1)} %convert_element_type.122, f32[1024,3072]{1,0:T(8,128)} %fusion.134, f32[1024,3072]{1,0:T(8,128)} %fusion.147, ...), kind=kOutput, calls=%fused_computation.21 | convolution fusion | flops 6709831680 | bytes 58785792 | tf_op jit(solution)/shard_map/dot_general | solution.py:135
  397.6 4.4 convolution_convert_fusion
  402.0 3.6 all-to-all-start.2
  405.7 26.2 %all-to-all-done.2 = bf16[32,16,1024]{2,1,0:T(8,128)(2,1)S(1)} async-done(((bf16[32,16,1024]{2,1,0:T(8,128)(2,1)}), bf16[32,16,1024]{2,1,0:T(8,128)(2,1)S(1)}, u32[]{:S(2)}, u32[]{:S(2)}) %all-to-all-start.2) | async-done | bytes 1048608 | tf_op jit(solution)/shard_map/all_to_all | solution.py:163
  436.4 3.4 fusion.25
  439.8 5.2 copy.144
  445.1 2.6 broadcast.157.clone
  447.7 209.4 %while.33 = (s32[]{:T(128)}, f32[16,1,512]{2,1,0:T(1,128)S(1)}, f32[16,2,512]{2,1,0:T(2,128)S(1)}, f32[64,16,2,512]{3,0,2,1:T(8,128)}, f32[64,16,2,512]{3,2,1,0:...) while((s32[]{:T(128)}, f32[16,1,512]{2,1,0:T(1,128)S(1)}, ...), condition=%wide.region_7.8_spmd.clone, body=%wide.region_5.7_spmd.clone.sunk | while | flops 90116 | bytes 753804 | solution.py:39
  657.2 9.1 fusion.149
  668.9 3.4 reshape.199
  672.3 4.1 fusion.72
  676.4 29.7 %all_to_all.58 = bf16[16,32,1024]{2,0,1:T(8,128)(2,1)S(1)} all-to-all(bf16[16,32,1024]{2,0,1:T(8,128)(2,1)S(1)} %get-tuple-element.288), channel_id=1, replica_groups=mesh['dp'=16,'fsdp'=2] {'dp','fsdp'}, dimensions={1} | all-to-all | bytes 2097152 | tf_op jit(solution)/shard_map/all_to_all | solution.py:169
  708.5 3.0 fusion.135
  711.7 8.0 fusion.150
  719.8 12.8 fusion.137
  732.7 10.3 multiply_convert_fusion.1
  743.0 2.7 copy-done.14
  745.7 9.7 fusion.133
  756.1 11.7 fusion.44
  767.8 12.2 fusion.148
  780.0 5.7 fusion.153
  785.7 64.4 %rev.7 = f32[16,512,256]{1,2,0:T(8,128)} reverse(f32[16,512,256]{1,2,0:T(8,128)} %fusion.153), dimensions={2} | reverse | bytes 16777216 | tf_op jit(solution)/shard_map/transpose(jvp())/rev | solution.py:31
  855.5 12.3 multiply_reduce_fusion.2
  867.8 18.2 %multiply_reduce_fusion = (f32[16,512]{1,0:T(8,128)}, f32[16,512]{1,0:T(8,128)S(1)}, f32[16,512]{1,0:T(8,128)S(1)}) fusion(f32[256]{0:T(256)S(1)} %copy-done.45, f32[16,512]{1,0:T(8,128)S(1)} %copy-done.28, f32[16,512,256]{1,2,0:T(8,128)S(1)} %fusion.151, f32[16,512]{1,0:T(8,128)S(1)} %copy-done.32, f32[16,512,256]{1,2,0:T(8,128)S(1)} %bitcast.161, ...), kind=kOutput, calls=%fused_computation.39 | convolution fusion | flops 6472835072 | bytes 21267456 | tf_op jit(solution)/shard_map/transpose(jvp(hnt,hns->hts))/dot_general | solution.py:26
  886.7 5.0 fusion.40
  891.8 3.1 convert_reduce_fusion.3
  894.9 40.1 %all-reduce.12 = (f32[1024]{0:T(1024)S(1)}, f32[1024]{0:T(1024)S(1)}, f32[3072]{0:T(1024)S(1)}, f32[512]{0:T(512)S(1)}, f32[3072]{0:T(1024)S(1)}, /*index=5*/f32[1024]{0:T(1024)S(1)}) all-reduce(f32[1024]{0:T(1024)S(1)} %get-tuple-element.232, ...), channel_id=2, replica_groups=mesh['dp'=16,'fsdp'=2] {'dp','fsdp'}, use_global_device_ids=true, to_apply=%region_11.12.clone | all-reduce | flops 9728 | bytes 77824
  938.5 26.9 %reduce-scatter.9.cloned.1.call-done = f32[16,3072]{1,0:T(8,128)} async-done(((f32[512,3072]{1,0:T(8,128)}), f32[16,3072]{1,0:T(8,128)}) %reduce-scatter.9.cloned.1.call-update) | async-done | bytes 196624 | tf_op jit(solution)/shard_map/reduce_scatter | solution.py:210
  965.4 161.2 %reduce-scatter.5.cloned.1.call-done = f32[32,3072]{1,0:T(8,128)} async-done(((f32[1024,3072]{1,0:T(8,128)}), f32[32,3072]{1,0:T(8,128)}) %reduce-scatter.5.cloned.1.call-update) | async-done | bytes 393232 | tf_op jit(solution)/shard_map/reduce_scatter | solution.py:206
  1126.6 162.2 %reduce-scatter.11.cloned.1.call-done = f32[96,1024]{1,0:T(8,128)} async-done(((f32[3072,1024]{1,0:T(8,128)}), f32[96,1024]{1,0:T(8,128)}) %reduce-scatter.11.cloned.1.call-update) | async-done | bytes 393232 | tf_op jit(solution)/shard_map/reduce_scatter | solution.py:212
  (560 shorter events, 348.3 us)
Async XLA Ops:
  7.2 60.2 %copy-start.3 = (bf16[1024,1024]{1,0:T(8,128)(2,1)S(1)}, bf16[1024,1024]{1,0:T(8,128)(2,1)}, u32[]{:S(2)}) copy-start(bf16[1024,1024]{1,0:T(8,128)(2,1)} %param.20) | copy-start | bytes 6291460
  7.2 60.1 %all-gather.7.cloned.1.call-start = ((), (), s32[]{:S(2)}) async-start(), calls=%async_computation.9 | async-start | bytes 1081344 | tf_op jit(solution)/shard_map/all_gather | solution.py:112
  7.9 322.4 %all-gather.9.cloned.1.call-start = ((), (), s32[]{:S(2)}) async-start(), calls=%async_computation.10 | async-start | bytes 3244032 | tf_op jit(solution)/shard_map/all_gather | solution.py:114
  8.7 330.3 %all-gather.11.cloned.1.call-start = ((), (), s32[]{:S(2)}) async-start(), calls=%async_computation.11 | async-start | bytes 6488064 | tf_op jit(solution)/shard_map/all_gather | solution.py:116
  56.8 19.1 %copy-start.39 = (f32[512]{0:T(512)}, f32[512]{0:T(512)S(1)}, u32[]{:S(2)}) copy-start(f32[512]{0:T(512)S(1)} %convert_element_type.123) | copy-start | bytes 6148
  61.1 19.2 %copy-start.29 = (f32[16,512]{1,0:T(8,128)S(1)}, f32[16,512]{1,0:T(8,128)}, u32[]{:S(2)}) copy-start(f32[16,512]{1,0:T(8,128)} %param.33) | copy-start | bytes 98308
  76.0 84.7 %all-to-all-start = ((bf16[32,16,1024]{2,1,0:T(8,128)(2,1)}), bf16[32,16,1024]{2,1,0:T(8,128)(2,1)S(1)}, u32[]{:S(2)}, u32[]{:S(2)}) async-start(bf16[32,16,1024]{2,1,0:T(8,128)(2,1)} %bitcast.169), calls=%async_computation | async-start | bytes 2097152 | tf_op jit(solution)/shard_map/all_to_all | solution.py:141
  79.7 271.5 %all-gather.5.cloned.1.call-start = ((), (), s32[]{:S(2)}) async-start(), calls=%async_computation.8 | async-start | bytes 6488064 | tf_op jit(solution)/shard_map/all_gather | solution.py:110
  80.3 204.4 %copy-start.44 = (f32[256]{0:T(256)}, f32[256]{0:T(256)S(1)}, u32[]{:S(2)}) copy-start(f32[256]{0:T(256)S(1)} %iota_convert_fusion) | copy-start | bytes 3076
  80.3 69.0 %copy-start.33 = (f32[16,512]{1,0:T(8,128)}, f32[16,512]{1,0:T(8,128)S(1)}, u32[]{:S(2)}) copy-start(f32[16,512]{1,0:T(8,128)S(1)} %get-tuple-element.292) | copy-start | bytes 98308
  80.3 204.4 %copy-start.27 = (f32[16,512]{1,0:T(8,128)}, f32[16,512]{1,0:T(8,128)S(1)}, u32[]{:S(2)}) copy-start(f32[16,512]{1,0:T(8,128)S(1)} %get-tuple-element.290) | copy-start | bytes 98308
  80.3 204.4 %copy-start.31 = (f32[16,512]{1,0:T(8,128)}, f32[16,512]{1,0:T(8,128)S(1)}, u32[]{:S(2)}) copy-start(f32[16,512]{1,0:T(8,128)S(1)} %get-tuple-element.289) | copy-start | bytes 98308
  84.8 64.5 %copy-start.48 = (f32[16,512]{1,0:T(8,128)S(1)}, f32[16,512]{1,0:T(8,128)}, u32[]{:S(2)}) copy-start(f32[16,512]{1,0:T(8,128)} %param.34) | copy-start | bytes 98308
  149.3 133.7 %copy-start.25 = (pred[256,256]{1,0:T(8,128)(4,1)}, pred[256,256]{1,0:T(8,128)(4,1)S(1)}, u32[]{:S(2)}) copy-start(pred[256,256]{1,0:T(8,128)(4,1)S(1)} %iota_compare_fusion) | copy-start | bytes 196612
  164.9 118.1 %copy-start.1 = (bf16[16,128,256]{2,1,0:T(8,128)(2,1)}, bf16[16,128,256]{2,1,0:T(8,128)(2,1)S(1)}, u32[]{:S(2)}) copy-start(bf16[16,128,256]{2,1,0:T(8,128)(2,1)S(1)} %reshape.192) | copy-start | bytes 3145732
  278.2 4.8 copy-start.16
  278.2 4.8 copy-start.4
  294.3 9.8 copy-start.46
  298.2 32.2 %all-to-all-start.1 = ((bf16[16,32,1024]{2,0,1:T(8,128)(2,1)}), bf16[16,32,1024]{2,0,1:T(8,128)(2,1)S(1)}, u32[]{:S(2)}, u32[]{:S(2)}) async-start(bf16[16,32,1024]{2,0,1:T(8,128)(2,1)} %fusion.69), calls=%async_computation.1 | async-start | bytes 2097152 | tf_op jit(solution)/shard_map/all_to_all | solution.py:145
  304.3 34.7 %copy-start.35 = (f32[1024]{0:T(1024)}, f32[1024]{0:T(1024)S(1)}, u32[]{:S(2)}) copy-start(f32[1024]{0:T(1024)S(1)} %fusion.128) | copy-start | bytes 12292
  330.3 8.6 copy-start.23
  351.1 46.4 %copy-start.47 = (bf16[512,3072]{1,0:T(8,128)(2,1)S(1)}, bf16[512,3072]{1,0:T(8,128)(2,1)}, u32[]{:S(2)}) copy-start(bf16[512,3072]{1,0:T(8,128)(2,1)} %all-gather.9.cloned.1.call-done) | copy-start | bytes 9437188
  397.6 4.5 copy-start.50
  402.0 34.3 %copy-start.28 = (f32[16,512]{1,0:T(8,128)S(1)}, f32[16,512]{1,0:T(8,128)}, u32[]{:S(2)}) copy-start(f32[16,512]{1,0:T(8,128)} %copy-done.27) | copy-start | bytes 98308
  402.0 34.3 %copy-start.32 = (f32[16,512]{1,0:T(8,128)S(1)}, f32[16,512]{1,0:T(8,128)}, u32[]{:S(2)}) copy-start(f32[16,512]{1,0:T(8,128)} %copy-done.31) | copy-start | bytes 98308
  402.0 34.3 %copy-start.45 = (f32[256]{0:T(256)S(1)}, f32[256]{0:T(256)}, u32[]{:S(2)}) copy-start(f32[256]{0:T(256)} %copy-done.44) | copy-start | bytes 3076
  402.0 34.4 %copy-start.49 = (f32[16,512]{1,0:T(8,128)S(1)}, f32[16,512]{1,0:T(8,128)}, u32[]{:S(2)}) copy-start(f32[16,512]{1,0:T(8,128)} %param.34) | copy-start | bytes 98308
  402.0 29.9 %all-to-all-start.2 = ((bf16[32,16,1024]{2,1,0:T(8,128)(2,1)}), bf16[32,16,1024]{2,1,0:T(8,128)(2,1)S(1)}, u32[]{:S(2)}, u32[]{:S(2)}) async-start(bf16[32,16,1024]{2,1,0:T(8,128)(2,1)} %bitcast.170), calls=%async_computation.2 | async-start | bytes 2097152 | tf_op jit(solution)/shard_map/all_to_all | solution.py:163
  405.7 532.8 %reduce-scatter.7.cloned.1.call-start = ((), (), s32[]{:S(2)}) async-start(), calls=%async_computation.13 | async-start | bytes 2162688 | tf_op jit(solution)/shard_map/reduce_scatter | solution.py:208
  436.4 229.9 %copy-start.11 = (bf16[16,128,256]{2,1,0:T(8,128)(2,1)}, bf16[16,128,256]{2,1,0:T(8,128)(2,1)S(1)}, u32[]{:S(2)}) copy-start(bf16[16,128,256]{2,1,0:T(8,128)(2,1)S(1)} %reshape.196) | copy-start | bytes 3145732
  657.2 9.1 copy-start.5
  657.2 9.1 copy-start.26
  668.9 3.4 copy-start.10
  668.9 3.4 copy-start.42
  672.3 33.8 %copy-start.18 = (f32[1024,512]{0,1:T(8,128)S(1)}, f32[1024,512]{0,1:T(8,128)}, u32[]{:S(2)}) copy-start(f32[1024,512]{0,1:T(8,128)} %get-tuple-element.294) | copy-start | bytes 6291460
  672.3 33.8 %copy-start.40 = (f32[512]{0:T(512)S(1)}, f32[512]{0:T(512)}, u32[]{:S(2)}) copy-start(f32[512]{0:T(512)} %copy-done.39) | copy-start | bytes 6148
  711.6 253.8 %reduce-scatter.9.cloned.1.call-start = ((), (), s32[]{:S(2)}) async-start(), calls=%async_computation.14 | async-start | bytes 6488064 | tf_op jit(solution)/shard_map/reduce_scatter | solution.py:210
  719.7 406.9 %reduce-scatter.5.cloned.1.call-start = ((), (), s32[]{:S(2)}) async-start(), calls=%async_computation.12 | async-start | bytes 12976128 | tf_op jit(solution)/shard_map/reduce_scatter | solution.py:206
  732.6 556.2 %reduce-scatter.11.cloned.1.call-start = ((), (), s32[]{:S(2)}) async-start(), calls=%async_computation.15 | async-start | bytes 12976128 | tf_op jit(solution)/shard_map/reduce_scatter | solution.py:212
  732.6 13.0 %copy-start.19 = (bf16[1024,1024]{1,0:T(8,128)(2,1)S(1)}, bf16[1024,1024]{1,0:T(8,128)(2,1)}, u32[]{:S(2)}) copy-start(bf16[1024,1024]{1,0:T(8,128)(2,1)} %param.21) | copy-start | bytes 6291460
  732.6 13.0 %copy-start.36 = (f32[1024]{0:T(1024)S(1)}, f32[1024]{0:T(1024)}, u32[]{:S(2)}) copy-start(f32[1024]{0:T(1024)} %copy-done.35) | copy-start | bytes 12292
  767.8 12.2 copy-start
  767.8 12.2 copy-start.2
  852.9 14.9 %slice-start = ((s8[8388608]{0:T(1024)(128)(4,1)}), s8[4194304]{0:T(1024)(128)(4,1)S(1)}, s32[]{:S(2)}) async-start(s8[8388608]{0:T(1024)(128)(4,1)} %bitcast.160), calls=%async_computation.16 | async-start | bytes 8388608
  855.5 12.3 slice-start.1
  867.8 18.2 %copy-start.30 = (f32[16,512]{1,0:T(8,128)S(1)}, f32[16,512]{1,0:T(8,128)}, u32[]{:S(2)}) copy-start(f32[16,512]{1,0:T(8,128)} %param.33) | copy-start | bytes 98308
  867.8 18.9 %copy-start.22 = (bf16[512,1024]{1,0:T(8,128)(2,1)S(1)}, bf16[512,1024]{1,0:T(8,128)(2,1)}, u32[]{:S(2)}) copy-start(bf16[512,1024]{1,0:T(8,128)(2,1)} %copy-done.21) | copy-start | bytes 3145732
  886.7 5.1 copy-start.20
  (16 other events, 36.6 us)
Sparse Core Ops, SparseCore 0:
  10.9 56.3 all-gather.6
  70.2 61.7 all-gather.8
  134.9 68.3 all-gather.10
  205.9 68.0 all-gather.4
  711.7 135.2 reduce-scatter.6
  854.1 111.3 reduce-scatter.8
  972.0 154.5 reduce-scatter.4
  1134.3 154.4 reduce-scatter.10
where the time goes:
time: 1320 us; the launch traced here: 1300 us
  waiting for transfers between devices  411 us (31%)
  local copies, waits for them, and re-layouts  315 us (24%)
  matrix products  224 us (17%)
  other arithmetic  203 us (15%)
  blocking collectives  112 us (8%)
  between operations  15.4 us (1%)
  starting transfers between devices  13.5 us (1%)
    reduce_scatter x1, waiting for transfers between devices, per_device(): lax.psum_scatter(grad_wfour, ('dp', 'fsdp'), scatter_dimension=0, tiled=T...  162 us
    reduce_scatter x1, waiting for transfers between devices, per_device(): lax.psum_scatter(grad_wone, ('dp', 'fsdp'), scatter_dimension=0, tiled=True)  161 us
    dynamic_update_slice x128, local copies, waits for them, and re-layouts, state_mix(): final_state, entering = lax.scan(advance, start, block_ends)  139 us
    rev x2, local copies, waits for them, and re-layouts, state_mix(): decay[:, :, ::-1]  129 us
    dot_general x10, matrix products, contract(): lax.dot_general(left, right, (((left_dim,), (right_dim,)), ((), ())), pre...  84.7 us
    unnamed x2, blocking collectives  82.5 us
    broadcast_in_dim x64, other arithmetic, state_mix(): final_state, entering = lax.scan(advance, start, block_ends)  65.6 us
    add x64, other arithmetic, advance(): return (state_in * carry_decay + contrib, state_in)  59 us
  transfers between devices with their start and end apart: 11, of which 6 were waited for; matrix products, arithmetic and copies ran while one was open for 34% of the time, Pallas kernels for 0%

commit v1 on v0

v1 whole, which is shorter than its diff:
```python
import functools

import jax
import jax.numpy as jnp
from jax import lax
from jax.experimental import pallas as pl
from jax.experimental.pallas import tpu as pltpu
from jax.sharding import PartitionSpec as P

SEQ = 16384
QBLK = 256
F32 = jnp.float32
BF = jnp.bfloat16
SWAP = [(0, 1), (1, 0)]


def mm(left, right, left_dim, right_dim):
    return lax.dot_general(
        left, right, (((left_dim,), (right_dim,)), ((), ())), preferred_element_type=F32
    )


def split(value):
    high = value.astype(BF)
    return high, (value - high.astype(F32)).astype(BF)


def decay_table(rate):
    row = lax.broadcasted_iota(jnp.int32, (8, rate.shape[1]), 0).astype(F32)
    table = jnp.exp(-rate * row)
    step = 8
    while step < QBLK:
        table = jnp.concatenate([table, table * jnp.exp(-rate * float(step))], axis=0)
        step *= 2
    return table


def shift_down(x, k):
    if k % 8 == 0:
        return jnp.concatenate([jnp.zeros((k, x.shape[1]), x.dtype), x[:-k]], axis=0)
    row = lax.broadcasted_iota(jnp.int32, x.shape, 0)
    return jnp.where(row >= k, pltpu.roll(x, k, 0), 0.0)


def shift_up(x, k):
    n = x.shape[0]
    if k % 8 == 0:
        return jnp.concatenate([x[k:], jnp.zeros((k, x.shape[1]), x.dtype)], axis=0)
    row = lax.broadcasted_iota(jnp.int32, x.shape, 0)
    return jnp.where(row < n - k, pltpu.roll(x, n - k, 0), 0.0)


def states(x, rate, shift):
    k = 1
    while k < x.shape[0]:
        x = x + shift(x, k) * jnp.exp(-rate * float(QBLK * k))
        k *= 2
    return shift(x, 1)


def flip_matrix():
    i = lax.broadcasted_iota(jnp.int32, (QBLK, QBLK), 0)
    j = lax.broadcasted_iota(jnp.int32, (QBLK, QBLK), 1)
    return jnp.where(i + j == QBLK - 1, 1.0, 0.0).astype(BF)


def toeplitz(kern, skip):
    rolled = pltpu.roll(jnp.broadcast_to(kern, (QBLK, QBLK)), 0, 1, stride=1, stride_axis=0)
    i = lax.broadcasted_iota(jnp.int32, (QBLK, QBLK), 0)
    j = lax.broadcasted_iota(jnp.int32, (QBLK, QBLK), 1)
    return jnp.where(j >= i, rolled, 0.0) + jnp.where(i == j, skip, 0.0)


def far_rows(entering, coeff, d_high, d_low):
    rows = entering.shape[0] + 8
    high, low = split(
        jnp.concatenate([entering, jnp.broadcast_to(coeff, (8, coeff.shape[1]))], axis=0)
    )
    both = mm(jnp.concatenate([high, low], axis=0), d_high, 1, 1)
    return both[:rows] + both[rows:] + mm(high, d_low, 1, 1)


def forward_channel(v, log_rate, coeff, skip, flip):
    count = v.shape[0]
    rate = jnp.exp(log_rate)
    d_high, d_low = split(decay_table(rate))
    v_flip = mm(v, flip, 1, 0).astype(BF)
    ends = mm(v_flip, d_high, 1, 0) + mm(v_flip, d_low, 1, 0)
    entering = states(ends, rate, shift_down)
    far = far_rows(entering * (coeff * jnp.exp(-rate)), coeff, d_high, d_low)
    t_high, t_low = split(toeplitz(far[count : count + 1], skip))
    return far[:count] + mm(v, t_high, 1, 0) + mm(v, t_low, 1, 0)


def forward_kernel(v_ref, lr_ref, co_ref, sk_ref, y_ref):
    flip = flip_matrix()
    for c in range(v_ref.shape[0]):
        y_ref[c] = forward_channel(
            v_ref[c], lr_ref[c], co_ref[c], sk_ref[c][:, :1], flip
        ).astype(BF)


def backward_channel(v, dy, log_rate, coeff, skip, flip):
    count = v.shape[0]
    rate = jnp.exp(log_rate)
    d_high, d_low = split(decay_table(rate))
    flipped = mm(jnp.concatenate([v, dy], axis=0), flip, 1, 0)
    v_flip, dy_flip = flipped[:count].astype(BF), flipped[count:].astype(BF)
    pair = jnp.concatenate([v_flip, dy], axis=0)
    lane = lax.broadcasted_iota(jnp.int32, (count, QBLK), 1).astype(F32)
    v_lag = (flipped[:count] * lane).astype(BF)
    dy_lag = (dy.astype(F32) * lane).astype(BF)
    sums = mm(jnp.concatenate([pair, v_lag, dy_lag], axis=0), d_high, 1, 0)
    lows = mm(pair, d_low, 1, 0)
    ends = sums[:count] + lows[:count]
    starts = sums[count : 2 * count] + lows[count:]
    ends_lag, starts_lag = sums[2 * count : 3 * count], sums[3 * count :]
    entering = states(ends, rate, shift_down)
    leaving = states(starts, rate, shift_up)
    one = jnp.exp(-rate)
    far = far_rows(leaving * (coeff * one), coeff, d_high, d_low)
    t_high, t_low = split(toeplitz(far[count : count + 1], skip))
    dv_flip = far[:count] + mm(dy_flip, t_high, 1, 0) + mm(dy_flip, t_low, 1, 0)
    dv = mm(dv_flip.astype(BF), flip, 1, 0)
    pairs = pltpu.roll(mm(v_flip, dy, 0, 0), 1, 1, stride=1, stride_axis=0)
    i = lax.broadcasted_iota(jnp.int32, (QBLK, QBLK), 0)
    j = lax.broadcasted_iota(jnp.int32, (QBLK, QBLK), 1)
    near = jnp.sum(jnp.where(j <= i, pairs, 0.0), axis=0, keepdims=True)
    lag = lax.broadcasted_iota(jnp.int32, (1, QBLK), 1).astype(F32)
    n_high, n_low = split(
        jnp.concatenate(
            [jnp.broadcast_to(near, (8, QBLK)), jnp.broadcast_to(near * lag, (8, QBLK))], axis=0
        )
    )
    both = mm(jnp.concatenate([n_high, n_low], axis=0), d_high, 1, 0)
    inner = both[:16] + both[16:] + mm(n_high, d_low, 1, 0)
    whole = jnp.exp(-rate * float(QBLK))
    outer = jnp.sum(entering * starts, axis=0, keepdims=True)
    moment = jnp.sum(
        ends_lag * leaving + entering * starts_lag + (float(QBLK) * whole) * (entering * leaving),
        axis=0,
        keepdims=True,
    )
    grad_coeff = inner[0:1] + one * outer
    grad_rate = -(coeff * rate) * (inner[8:9] + one * (moment + outer))
    return dv, grad_rate, grad_coeff, near[:, :1]


def backward_kernel(v_ref, dy_ref, lr_ref, co_ref, sk_ref, dv_ref, gr_ref, gc_ref, gs_ref):
    flip = flip_matrix()
    for c in range(v_ref.shape[0]):
        dv, grad_rate, grad_coeff, grad_skip = backward_channel(
            v_ref[c], dy_ref[c], lr_ref[c], co_ref[c], sk_ref[c][:, :1], flip
        )
        dv_ref[c] = dv.astype(BF)
        gr_ref[c] = grad_rate
        gc_ref[c] = grad_coeff
        gs_ref[c] = jnp.broadcast_to(grad_skip, (1, 128))


def mixer_call(kernel, tokens_in, params, token_outs, grads, name):
    chans, count, _ = tokens_in[0].shape
    per = 4
    n = params[0].shape[2]
    wide = pl.BlockSpec((per, count, QBLK), lambda i: (i, 0, 0))
    row = pl.BlockSpec((per, 1, n), lambda i: (i, 0, 0))
    lane = pl.BlockSpec((per, 1, 128), lambda i: (i, 0, 0))
    out_specs = [wide] * token_outs
    out_shape = [jax.ShapeDtypeStruct((chans, count, QBLK), BF)] * token_outs
    if grads:
        out_specs += [row, row, lane]
        out_shape += [jax.ShapeDtypeStruct((chans, 1, n), F32)] * 2
        out_shape += [jax.ShapeDtypeStruct((chans, 1, 128), F32)]
    return pl.pallas_call(
        kernel,
        grid=(chans // per,),
        in_specs=[wide] * len(tokens_in) + [row, row, lane],
        out_specs=out_specs,
        out_shape=out_shape,
        compiler_params=pltpu.CompilerParams(vmem_limit_bytes=48 * 2**20),
        name=name,
    )(*tokens_in, *params)


def swap_cores(x):
    return lax.ppermute(x, "fsdp", SWAP)


def across(x, size, bit):
    return lax.ppermute(x, "dp", [(i, i ^ (1 << bit)) for i in range(size)])


def bit_of(bit):
    return (lax.axis_index("dp") >> bit) & 1


def gather_bits(x, size, order, layout):
    have = []
    for bit in order:
        other = across(x, size, bit)
        mine = bit_of(bit) == 1
        have = [b for b in layout if b in have or b == bit]
        x = jnp.stack(
            [jnp.where(mine, other, x), jnp.where(mine, x, other)], axis=have.index(bit)
        )
    return x


def scatter_bits(x, size, order, layout, send_type):
    have = list(layout)
    for bit in order:
        axis = have.index(bit)
        mine = bit_of(bit)
        theirs = lax.dynamic_index_in_dim(x, 1 - mine, axis, keepdims=False)
        kept = lax.dynamic_index_in_dim(x, mine, axis, keepdims=False)
        x = kept + across(theirs.astype(send_type), size, bit).astype(F32)
        have.remove(bit)
    return x


def gelu_slope(hidden):
    return (
        0.5 * (1.0 + lax.erf(hidden * 0.7071067811865476))
        + hidden * jnp.exp(-0.5 * hidden * hidden) * 0.3989422804014327
    )


def per_device(
    size,
    tokens,
    cotangent,
    lengths,
    norm_gain,
    norm_bias,
    w_one,
    b_one,
    w_two,
    b_two,
    w_three,
    b_three,
    w_four,
    b_four,
    log_rate,
    ssm_coeff,
    ssm_skip,
):
    bits = size.bit_length() - 1
    tok_dev, width = tokens.shape
    rows_e = w_one.shape[0]
    rows_f = w_four.shape[0]
    rows_h = w_three.shape[0]
    f_half = size * rows_f
    h_half = size * rows_h
    buckets = lengths.shape[0]
    group = size // buckets
    group_bits = group.bit_length() - 1
    natural = list(range(bits))[::-1]
    by_owner = natural[bits - group_bits :] + natural[: bits - group_bits]
    top = natural[: bits - group_bits]
    order_a = list(range(2, bits)) + [0, 1]
    order_b = list(range(2, bits)) + [1, 0]
    core = lax.axis_index("fsdp")
    first = core == 0
    chip = lax.axis_index("dp")

    def natural_pair(mine, other, axis=0):
        return jnp.stack(
            [jnp.where(first, mine, other), jnp.where(first, other, mine)], axis=axis
        )

    def halves_f(x):
        parts = x.reshape(x.shape[:-1] + (size, 2, rows_f))
        a, b = parts[..., 0, :], parts[..., 1, :]
        shape = x.shape[:-1] + (f_half,)
        return (
            jnp.where(first, a, b).reshape(shape),
            jnp.where(first, b, a).reshape(shape),
        )

    def halves_h(x):
        parts = x.reshape(x.shape[:-1] + (buckets, group, 2, rows_h))
        parts = jnp.moveaxis(parts, -4, -3)
        a, b = parts[..., 0, :], parts[..., 1, :]
        shape = x.shape[:-1] + (h_half,)
        return (
            jnp.where(first, a, b).reshape(shape),
            jnp.where(first, b, a).reshape(shape),
        )

    tok_pair = jnp.concatenate([tokens, swap_cores(tokens)], axis=0)
    cot_pair = jnp.concatenate([cotangent, swap_cores(cotangent)], axis=0)

    two_mine, two_other = halves_h(w_two)
    vec = jnp.concatenate([norm_gain, norm_bias, b_four, b_one, b_three, b_two])
    vec_len = vec.shape[0]
    vec_rows = -(-2 * vec_len // h_half)
    two_got, vec_got = swap_cores(two_other), swap_cores(vec)
    two_rows = natural_pair(two_mine, two_got).reshape(2 * rows_e, h_half)
    vec_both = jnp.pad(
        natural_pair(vec, vec_got).reshape(-1), (0, vec_rows * h_half - 2 * vec_len)
    ).reshape(vec_rows, h_half)
    small = gather_bits(
        jnp.concatenate([two_rows, vec_both], axis=0), size, order_a, natural
    ).reshape(size, 2 * rows_e + vec_rows, h_half)
    two_half = small[:, : 2 * rows_e].reshape(width, h_half)
    vecs = (
        small[:, 2 * rows_e :]
        .reshape(size, -1)[:, : 2 * vec_len]
        .reshape(size, 2, vec_len)
        .astype(F32)
    )
    gain_f = vecs[:, :, :rows_e].reshape(1, width)
    nbias_f = vecs[:, :, rows_e : 2 * rows_e].reshape(1, width)
    bfour_f = vecs[:, :, 2 * rows_e : 3 * rows_e].reshape(1, width)
    own_vecs = jnp.where(first, vecs[:, 0], vecs[:, 1])
    bone_f = own_vecs[:, 3 * rows_e : 3 * rows_e + rows_f].reshape(1, f_half)
    bthree_f = own_vecs[:, 3 * rows_e + rows_f : 3 * rows_e + 2 * rows_f].reshape(1, f_half)
    btwo_f = (
        own_vecs[:, 3 * rows_e + 2 * rows_f :]
        .reshape(buckets, group, rows_h)
        .swapaxes(0, 1)
        .reshape(h_half, 1)
    )

    one_mine, one_other = halves_f(w_one)
    three_mine, three_other = halves_f(w_three)
    one_got, three_got = swap_cores(one_other), swap_cores(three_other)
    one_rows = natural_pair(one_mine, one_got)
    one_half = jnp.stack(
        [
            gather_bits(one_rows[0], size, order_a, natural),
            gather_bits(one_rows[1], size, order_b, natural),
        ],
        axis=bits,
    ).reshape(width, f_half)
    three_half = jnp.stack(
        [
            gather_bits(three_mine, size, order_a, by_owner),
            gather_bits(three_got, size, order_b, by_owner),
        ]
    ).reshape(2 * h_half, f_half)
    four_rows = w_four.reshape(2, rows_f // 2, width)
    four_half = jnp.stack(
        [
            gather_bits(four_rows[0], size, order_a, natural),
            gather_bits(four_rows[1], size, order_b, natural),
        ],
        axis=bits,
    ).reshape(f_half, width)

    def shared(x):
        return gather_bits(x, size, sorted(top), top).reshape((buckets * rows_h,) + x.shape[1:])

    params = shared(
        jnp.concatenate(
            [log_rate, ssm_coeff, jnp.broadcast_to(ssm_skip[:, None], (rows_h, 128))], axis=1
        )
    )[:, None]
    nstate = log_rate.shape[1]
    mix_params = (
        params[..., :nstate],
        params[..., nstate : 2 * nstate],
        params[..., 2 * nstate :],
    )
    chans = buckets * rows_h
    tok_chip = 2 * tok_dev
    per_dev = tok_dev // QBLK
    groups = [[b * group + j for j in range(group)] for b in range(buckets)]

    def exchange(x):
        return lax.all_to_all(x, "dp", split_axis=0, concat_axis=0, axis_index_groups=groups)

    def to_owner(x):
        got = exchange(x.reshape(group, chans, tok_chip)).reshape(
            group, chans, 2, per_dev, QBLK
        )
        got = jnp.where(first, got, got[:, :, ::-1])
        return got.swapaxes(0, 1).reshape(chans, group * 2 * per_dev, QBLK)

    def from_owner(x):
        parts = x.reshape(chans, group, 2, per_dev, QBLK).swapaxes(0, 1)
        parts = jnp.where(first, parts, parts[:, :, ::-1])
        return exchange(parts.reshape(group, chans, tok_chip)).reshape(h_half, tok_chip)

    def swap_turned(x):
        got = swap_cores(x)
        return jnp.concatenate([got[:, tok_dev:], got[:, :tok_dev]], axis=1)

    device = 2 * chip + core
    place_own = device * tok_dev + jnp.arange(tok_dev, dtype=jnp.int32)
    place_other = (device ^ 1) * tok_dev + jnp.arange(tok_dev, dtype=jnp.int32)
    place = jnp.concatenate([place_own, place_other])
    bucket_range = jnp.arange(buckets, dtype=jnp.int32)
    limit = jnp.sum(
        jnp.where((place // SEQ)[:, None] == bucket_range[None, :], lengths[None, :], 0), axis=1
    )
    live = (place % SEQ < limit).astype(F32)[:, None]

    inputs = tok_pair.astype(F32)
    centered = inputs - jnp.mean(inputs, axis=-1, keepdims=True)
    inv_std = lax.rsqrt(jnp.mean(centered * centered, axis=-1, keepdims=True) + 1e-05)
    normal_hat = centered * inv_std
    normed = (normal_hat * gain_f + nbias_f).astype(BF)
    out_grad = (live * cot_pair.astype(F32)).astype(BF)
    hidden_two_t = mm(two_half, normed, 0, 1) + btwo_f
    reduced_t = jax.nn.gelu(hidden_two_t, approximate=False).astype(BF)
    v_seq = to_owner(reduced_t)
    (y_seq,) = mixer_call(forward_kernel, [v_seq], mix_params, 1, False, "mixer_forward")
    y_own = from_owner(y_seq)
    y_t = jnp.concatenate([y_own, swap_turned(y_own)], axis=0)

    hidden_one = jnp.dot(normed, one_half, preferred_element_type=F32) + bone_f
    act_one = jax.nn.gelu(hidden_one, approximate=False)
    gate = mm(y_t, three_half, 0, 0) + bthree_f
    product = (act_one * gate).astype(BF)
    grad_four = mm(product, out_grad, 0, 0)
    branch = jnp.dot(product, four_half, preferred_element_type=F32)
    branch_own = branch[:tok_dev] + swap_cores(branch[tok_dev:].astype(BF)).astype(F32)
    mixed = (live[:tok_dev] * (inputs[:tok_dev] + branch_own + bfour_f)).astype(BF)

    prod_grad = mm(out_grad, four_half, 1, 1)
    gate_grad = (prod_grad * act_one).astype(BF)
    dy_part = mm(three_half, gate_grad, 1, 1)
    dy_own = (
        dy_part[:h_half] + swap_turned(dy_part[h_half:].astype(BF)).astype(F32)
    ).astype(BF)
    dy_seq = to_owner(dy_own)
    dv_seq, grad_rate, grad_coeff, grad_skip = mixer_call(
        backward_kernel, [v_seq, dy_seq], mix_params, 1, True, "mixer_backward"
    )
    dv_own = from_owner(dv_seq)
    mix_grads = jnp.concatenate([grad_rate[:, 0], grad_coeff[:, 0], grad_skip[:, 0]], axis=1)
    mix_grads = scatter_bits(
        mix_grads.reshape((2,) * len(top) + (rows_h, -1)), size, sorted(top)[::-1], top, F32
    )

    act_grad = prod_grad * gate
    one_grad = (act_grad * gelu_slope(hidden_one)).astype(BF)
    two_grad_t = (dv_own.astype(F32) * gelu_slope(hidden_two_t)).astype(BF)
    grad_three = mm(y_t, gate_grad, 1, 0)
    grad_one = mm(normed, one_grad, 0, 0)
    grad_two = mm(normed, two_grad_t, 0, 1)
    normed_part = mm(one_grad, one_half, 1, 1) + mm(two_grad_t, two_half, 0, 1)
    normed_grad = normed_part[:tok_dev] + swap_cores(normed_part[tok_dev:].astype(BF)).astype(
        F32
    )
    hat = normal_hat[:tok_dev]
    hat_grad = normed_grad * gain_f
    input_grad = (
        out_grad[:tok_dev].astype(F32)
        + inv_std[:tok_dev]
        * (
            hat_grad
            - jnp.mean(hat_grad, axis=-1, keepdims=True)
            - hat * jnp.mean(hat_grad * hat, axis=-1, keepdims=True)
        )
    ).astype(BF)

    shape_bits = (2,) * bits
    back_a, back_b = order_a[::-1], order_b[::-1]

    def merge_f(mine, other):
        rows = mine.shape[0]
        parts = (mine.reshape(rows, size, rows_f), other.reshape(rows, size, rows_f))
        return natural_pair(*parts, axis=2).reshape(rows, 2 * f_half)

    four_parts = grad_four.reshape(shape_bits + (2, rows_f // 2, width))
    four_a, four_b = four_parts[..., 0, :, :], four_parts[..., 1, :, :]
    sum_four = jnp.concatenate(
        [
            scatter_bits(four_a, size, back_a, natural, BF),
            scatter_bits(four_b, size, back_b, natural, BF),
        ],
        axis=0,
    )
    three_parts = grad_three.reshape((2,) + shape_bits + (rows_h, f_half))
    three_own = scatter_bits(three_parts[0], size, back_a, by_owner, BF)
    three_for = scatter_bits(three_parts[1], size, back_b, by_owner, BF)
    sum_three = merge_f(three_own, swap_cores(three_for))
    one_parts = grad_one.reshape(shape_bits + (2, rows_e, f_half))
    one_a = scatter_bits(one_parts[..., 0, :, :], size, back_a, natural, BF)
    one_b = scatter_bits(one_parts[..., 1, :, :], size, back_b, natural, BF)
    sum_one = merge_f(
        jnp.where(first, one_a, one_b), swap_cores(jnp.where(first, one_b, one_a))
    )

    def chipwise(x):
        return x.reshape(size, -1)

    grad_btwo = (
        jnp.sum(two_grad_t.astype(F32), axis=1)
        .reshape(group, buckets, rows_h)
        .swapaxes(0, 1)
    )
    both_cores = jnp.concatenate(
        [
            chipwise(jnp.sum(normed_grad * hat, axis=0)),
            chipwise(jnp.sum(normed_grad, axis=0)),
            chipwise(jnp.sum(out_grad[:tok_dev].astype(F32), axis=0)),
        ],
        axis=1,
    )
    one_core = jnp.concatenate(
        [
            chipwise(jnp.sum(one_grad.astype(F32), axis=0)),
            chipwise(jnp.sum(gate_grad.astype(F32), axis=0)),
            chipwise(grad_btwo),
        ],
        axis=1,
    )
    vec_grads = jnp.concatenate([both_cores, one_core], axis=1)
    grad_rows = -(-vec_grads.shape[1] // h_half)
    vec_grads = jnp.pad(vec_grads, ((0, 0), (0, grad_rows * h_half - vec_grads.shape[1])))
    small_grads = jnp.concatenate(
        [grad_two.reshape(size, 2 * rows_e, h_half), vec_grads.reshape(size, grad_rows, h_half)],
        axis=1,
    ).reshape(shape_bits + (2 * rows_e + grad_rows, h_half))
    small_sum = scatter_bits(small_grads, size, back_a, natural, BF)
    two_a, two_b = small_sum[:rows_e], small_sum[rows_e : 2 * rows_e]
    vec_sum = small_sum[2 * rows_e :].reshape(-1)
    shared_sum = vec_sum[: 6 * rows_e].reshape(3, 2, rows_e)
    for_me = jnp.where(first, shared_sum[:, 0], shared_sum[:, 1])
    for_other = jnp.where(first, shared_sum[:, 1], shared_sum[:, 0])
    for_me = for_me + swap_cores(for_other)
    own_sum = vec_sum[6 * rows_e :]
    two_mine_sum = jnp.where(first, two_a, two_b)
    two_other_sum = swap_cores(jnp.where(first, two_b, two_a))
    parts = (
        two_mine_sum.reshape(rows_e, group, buckets, rows_h),
        two_other_sum.reshape(rows_e, group, buckets, rows_h),
    )
    sum_two = natural_pair(*parts, axis=3).swapaxes(1, 2).reshape(rows_e, 2 * h_half)

    return (
        mixed,
        input_grad,
        for_me[0],
        for_me[1],
        sum_one,
        own_sum[:rows_f],
        sum_two,
        own_sum[2 * rows_f : 2 * rows_f + rows_h],
        sum_three,
        own_sum[rows_f : 2 * rows_f],
        sum_four,
        for_me[2],
        mix_grads[:, :nstate],
        mix_grads[:, nstate : 2 * nstate],
        mix_grads[:, 2 * nstate],
    )


def solution(mesh):
    both = ("dp", "fsdp")
    rows, vector = P(both, None), P(both)
    in_specs = (
        rows, rows, P(), vector, vector, rows, vector, rows, vector, rows, vector, rows, vector,
        rows, rows, vector,
    )
    out_specs = (
        rows, rows, vector, vector, rows, vector, rows, vector, rows, vector, rows, vector,
        rows, rows, vector,
    )
    return jax.shard_map(
        functools.partial(per_device, mesh.shape["dp"]),
        mesh=mesh,
        in_specs=in_specs,
        out_specs=out_specs,
        check_vma=False,
    )
```

time: 1320 us -> 642 us (0.49); the launches traced: 1300 us -> 634 us
  waiting for transfers between devices: 411 us -> 163 us
  local copies, waits for them, and re-layouts: 315 us -> 72.5 us
  blocking collectives: 112 us -> 0 us
  other arithmetic: 203 us -> 98.7 us
  matrix products: 224 us -> 136 us
  starting transfers between devices: 13.5 us -> 93.3 us
  Pallas kernels: 0 us -> 66.6 us
    reduce_scatter x4 -> x0, waiting for transfers between devices: 350 us -> none  [the longest x1 162 us: per_device(): lax.psum_scatter(grad_wfour, ('dp', 'fsdp'), scatter_dimension=0, tiled=T...]
    ppermute x0 -> x72, waiting for transfers between devices: none -> 162 us  [the longest x58 161 us: across(): return lax.ppermute(x, 'dp', [(i, i ^ 1 << bit) for i in range(size)])]
    dynamic_update_slice x128 -> x0, local copies, waits for them, and re-layouts: 139 us -> none  [state_mix(): final_state, entering = lax.scan(advance, start, block_ends)]
    rev x2 -> x0, local copies, waits for them, and re-layouts: 129 us -> none  [state_mix(): decay[:, :, ::-1]]
    dot_general x24 -> x12, matrix products: 224 us -> 136 us  [the longest x10 82.8 us: mm(): lax.dot_general(left, right, (((left_dim,), (right_dim,)), ((), ())), pre...]
    unnamed x2 -> x0, blocking collectives: 82.5 us -> none
    ppermute x0 -> x72, starting transfers between devices: none -> 76.6 us  [the longest x58 74 us: across(): return lax.ppermute(x, 'dp', [(i, i ^ 1 << bit) for i in range(size)])]
    pallas_call x0 -> x2, Pallas kernels: none -> 66.6 us  [mixer_call(): pl.pallas_call(kernel, grid=(chans // per,), in_specs=[wide] * len(tokens...]
  transfers between devices with their start and end apart: 11 -> 76, of which waited for: 6 -> 29; matrix products, arithmetic and copies ran while one was open for 34% -> 26% of each run, Pallas kernels for 0% -> 11%
where the time goes in v1:
time: 642 us; the launch traced here: 634 us
  waiting for transfers between devices  163 us (25%)
  matrix products  136 us (21%)
  other arithmetic  98.7 us (15%)
  starting transfers between devices  93.3 us (15%)
  local copies, waits for them, and re-layouts  72.5 us (11%)
  Pallas kernels  66.6 us (10%)
    ppermute x58, waiting for transfers between devices, across(): return lax.ppermute(x, 'dp', [(i, i ^ 1 << bit) for i in range(size)])  161 us
    dot_general x10, matrix products, mm(): lax.dot_general(left, right, (((left_dim,), (right_dim,)), ((), ())), pre...  82.8 us
    ppermute x58, starting transfers between devices, across(): return lax.ppermute(x, 'dp', [(i, i ^ 1 << bit) for i in range(size)])  74 us
    pallas_call x2, Pallas kernels, mixer_call(): pl.pallas_call(kernel, grid=(chans // per,), in_specs=[wide] * len(tokens...  66.6 us
    dot_general x1, matrix products, per_device(): hidden_one = jnp.dot(normed, one_half, preferred_element_type=F32) + bone_f  44.6 us
    another operation x50, other arithmetic, gather_bits(): jnp.stack([jnp.where(mine, other, x), jnp.where(mine, x, other)], axis=ha...  25.2 us
    all_to_all x4, starting transfers between devices, exchange(): lax.all_to_all(x, 'dp', split_axis=0, concat_axis=0, axis_index_groups=gr...  16.6 us
    add x26, other arithmetic, scatter_bits(): x = kept + across(theirs.astype(send_type), size, bit).astype(F32)  14.3 us
  transfers between devices with their start and end apart: 76, of which 29 were waited for; matrix products, arithmetic and copies ran while one was open for 26% of the time, Pallas kernels for 11%

profile of v1, /device:TPU:0, one launch (start us, length us, event | category | flops | bytes accessed | tf_op | source)
XLA Modules:
  0.0 633.7 jit_solution(1197802433810484451)
XLA Ops:
  4.1 4.1 concatenate.76
  10.3 4.0 collective-permute-start.16
  37.8 8.0 %collective-permute-done.19 = bf16[2,16,1536]{2,1,0:T(8,128)(2,1)S(1)} collective-permute-done((bf16[2,16,1536]{2,1,0:T(8,128)(2,1)S(1)}, bf16[2,16,1536]{2,1,0:T(8,128)(2,1)S(1)}, u32[]{:S(2)}, u32[]{:S(2)}) %collective-permute-start.19) | collective-permute-done | bytes 98336 | tf_op jit(solution)/shard_map/ppermute | solution.py:190
  49.4 4.2 collective-permute-done.31
  59.2 9.7 %collective-permute-done.13 = bf16[2,32,1536]{2,1,0:T(8,128)(2,1)S(1)} collective-permute-done((bf16[2,32,1536]{2,1,0:T(8,128)(2,1)S(1)}, bf16[2,32,1536]{2,1,0:T(8,128)(2,1)S(1)}, u32[]{:S(2)}, u32[]{:S(2)}) %collective-permute-start.13) | collective-permute-done | bytes 196640 | tf_op jit(solution)/shard_map/ppermute | solution.py:190
  76.4 8.1 %collective-permute-done.32 = bf16[2,48,1024]{2,1,0:T(8,128)(2,1)S(1)} collective-permute-done((bf16[2,48,1024]{2,1,0:T(8,128)(2,1)S(1)}, bf16[2,48,1024]{2,1,0:T(8,128)(2,1)S(1)}, u32[]{:S(2)}, u32[]{:S(2)}) %collective-permute-start.32) | collective-permute-done | bytes 196640 | tf_op jit(solution)/shard_map/ppermute | solution.py:190
  121.9 5.5 subtract_multiply_fusion
  127.4 6.9 %fusion.22 = (bf16[256,2048]{1,0:T(8,128)(2,1)}, f32[256,2048]{1,0:T(8,128)}) fusion(f32[256]{0:T(256)S(1)} %add.348, bf16[1024,256]{1,0:T(8,128)(2,1)S(1)} %bitcast.410, bf16[2048,1024]{1,0:T(8,128)(2,1)S(1)} %get-tuple-element.102), kind=kOutput, calls=%fused_computation.57 | convolution fusion | flops 1108344832 | bytes 7865344 | tf_op jit(solution)/shard_map/dot_general | solution.py:18
  134.4 3.6 all-to-all-start
  147.8 13.4 %collective-permute-done.11 = bf16[2,2,2,32,1536]{4,3,1,0,2:T(8,128)(2,1)} collective-permute-done((bf16[2,2,2,32,1536]{4,3,1,0,2:T(8,128)(2,1)}, bf16[2,2,2,32,1536]{4,3,1,0,2:T(8,128)(2,1)}, u32[]{:S(2)}, u32[]{:S(2)}) %collective-permute-start.11) | collective-permute-done | bytes 786464 | tf_op jit(solution)/shard_map/ppermute | solution.py:190
  168.4 20.0 %mixer_forward.1 = bf16[32,64,256]{2,1,0:T(8,128)(2,1)S(1)} custom-call(bf16[32,64,256]{2,1,0:T(8,128)(2,1)S(1)} %reshape.529.v_ref, f32[32,1,512]{2,1,0:T(1,128)S(1)} %get-tuple-element.175.lr_ref, f32[32,1,512]{2,1,0:T(1,128)S(1)} %get-tuple-element.174.co_ref, f32[32,1,128]{2,1,0:T(1,128)S(1)} %slice.268.sk_ref), custom_call_target="tpu_custom_call" | custom-call | tf_op jit(solution)/shard_map/mixer_forward/pallas_call | solution.py:174
  191.9 4.6 all-to-all-start.1
  204.0 3.9 multiply_convert_fusion.2
  208.6 12.5 %fusion.108 = f32[2048,1536]{1,0:T(8,128)} fusion(bf16[2048,1024]{1,0:T(8,128)(2,1)} %multiply_convert_fusion.2, bf16[1536,1024]{1,0:T(8,128)(2,1)} %bitcast.408), kind=kOutput, calls=%fused_computation.369 | convolution fusion | flops 6442450944 | bytes 19922944 | tf_op jit(solution)/shard_map/dot_general | solution.py:18
  221.1 4.4 fusion.89
  225.7 5.0 fusion.49
  230.7 44.6 %convert_reduce_fusion.1 = (f32[1536]{0:T(1024)S(1)}, bf16[2048,1536]{1,0:T(8,128)(2,1)}, f32[1536]{0:T(1024)S(1)}, bf16[2048,1536]{1,0:T(8,128)(2,1)}, f32[2048,1536]{1,0:T(8,128)S(1)}) fusion(f32[1536]{0:T(1024)S(1)} %copy-done.102, f32[2048,1536]{1,0:T(8,128)} %fusion.108, f32[2048,1536]{1,0:T(8,128)S(1)} %fusion.49, f32[1536]{0:T(1024)S(1)} %add.351, ...), kind=kOutput, calls=%fused_computation.11 | convolution fusion | flops 6703543296 | bytes 57696256 | tf_op jit(solution)/shard_map/dot_general | solution.py:412
  275.3 7.8 %fusion.110 = f32[512,2048]{1,0:T(8,128)} fusion(bf16[512,1536]{1,0:T(8,128)(2,1)S(1)} %bitcast.413, bf16[2048,1536]{1,0:T(8,128)(2,1)} %get-tuple-element.95), kind=kOutput, calls=%fused_computation.371 | convolution fusion | flops 3221225472 | bytes 12058624 | tf_op jit(solution)/shard_map/dot_general | solution.py:18
  283.0 8.3 %fusion.48 = f32[512,1536]{1,0:T(8,128)} fusion(bf16[2048,1536]{1,0:T(8,128)(2,1)} %get-tuple-element.95, bf16[256,1024]{1,0:T(8,128)(2,1)} %copy-done.81, bf16[256,1024]{1,0:T(8,128)(2,1)S(1)} %get-tuple-element.119, bf16[256,2048]{1,0:T(8,128)(2,1)} %bitcast.45), kind=kOutput, calls=%fused_computation.116 | convolution fusion | flops 3227516928 | bytes 11534336 | tf_op jit(solution)/shard_map/dot_general | solution.py:18
  291.4 10.7 %fusion.109 = f32[2048,1024]{1,0:T(8,128)} fusion(bf16[2048,1536]{1,0:T(8,128)(2,1)} %get-tuple-element.93, bf16[1024,1536]{1,0:T(8,128)(2,1)S(1)} %bitcast.407), kind=kOutput, calls=%fused_computation.370 | convolution fusion | flops 6442450944 | bytes 17825792 | tf_op jit(solution)/shard_map/dot_general | solution.py:18
  302.1 11.9 %fusion.112 = f32[1024,1536]{1,0:T(8,128)} fusion(bf16[2048,1024]{1,0:T(8,128)(2,1)} %copy-done.24, bf16[2048,1536]{1,0:T(8,128)(2,1)} %get-tuple-element.93), kind=kOutput, calls=%fused_computation.373 | convolution fusion | flops 6442450944 | bytes 16777216 | tf_op jit(solution)/shard_map/dot_general | solution.py:18
  314.0 5.5 multiply_convert_fusion.1
  319.5 10.4 %fusion.113 = f32[1536,1024]{1,0:T(8,128)S(1)} fusion(bf16[2048,1536]{1,0:T(8,128)(2,1)} %multiply_convert_fusion.1, bf16[2048,1024]{1,0:T(8,128)(2,1)} %multiply_convert_fusion.2), kind=kOutput, calls=%fused_computation.374 | convolution fusion | flops 6442450944 | bytes 16777216 | tf_op jit(solution)/shard_map/dot_general | solution.py:18
  330.0 9.1 %fusion.107 = f32[2048,1024]{1,0:T(8,128)} fusion(bf16[2048,1536]{1,0:T(8,128)(2,1)S(1)} %copy-done.17, bf16[1536,1024]{1,0:T(8,128)(2,1)S(1)} %bitcast.409), kind=kOutput, calls=%fused_computation.368 | convolution fusion | flops 6442450944 | bytes 17825792 | tf_op jit(solution)/shard_map/dot_general | solution.py:417
  357.0 4.0 slice.364
  361.2 12.5 %collective-permute-done.58 = bf16[2,2,2,16,1536]{4,3,2,1,0:T(8,128)(2,1)} collective-permute-done((bf16[2,2,2,16,1536]{4,3,2,1,0:T(8,128)(2,1)}, bf16[2,2,2,16,1536]{4,3,2,1,0:T(8,128)(2,1)}, u32[]{:S(2)}, u32[]{:S(2)}) %collective-permute-start.58) | collective-permute-done | bytes 393248 | tf_op jit(solution)/shard_map/ppermute | solution.py:190
  378.1 4.0 collective-permute-done.59
  382.7 13.6 %collective-permute-done.55 = bf16[2,2,16,1536]{3,2,0,1:T(8,128)(2,1)S(1)} collective-permute-done((bf16[2,2,16,1536]{3,2,0,1:T(8,128)(2,1)S(1)}, bf16[2,2,16,1536]{3,2,0,1:T(8,128)(2,1)S(1)}, u32[]{:S(2)}, u32[]{:S(2)}) %collective-permute-start.55) | collective-permute-done | bytes 196640 | tf_op jit(solution)/shard_map/ppermute | solution.py:190
  396.8 6.0 collective-permute-done.60
  402.9 6.5 %collective-permute-done.56 = bf16[2,16,1536]{2,1,0:T(8,128)(2,1)S(1)} collective-permute-done((bf16[2,16,1536]{2,1,0:T(8,128)(2,1)S(1)}, bf16[2,16,1536]{2,1,0:T(8,128)(2,1)S(1)}, u32[]{:S(2)}, u32[]{:S(2)}) %collective-permute-start.56) | collective-permute-done | bytes 98336 | tf_op jit(solution)/shard_map/ppermute | solution.py:190
  409.4 4.0 collective-permute-done.61
  414.4 13.5 %collective-permute-done.44 = bf16[2,2,2,32,1536]{4,3,1,0,2:T(8,128)(2,1)S(1)} collective-permute-done((bf16[2,2,2,32,1536]{4,3,1,0,2:T(8,128)(2,1)S(1)}, bf16[2,2,2,32,1536]{4,3,1,0,2:T(8,128)(2,1)S(1)}, u32[]{:S(2)}, u32[]{:S(2)}) %collective-permute-start.44) | collective-permute-done | bytes 786464 | tf_op jit(solution)/shard_map/ppermute | solution.py:190
  444.8 4.5 all-to-all-start.2
  456.0 4.7 collective-permute-done.49
  462.6 6.4 %collective-permute-start.50 = (bf16[2,32,1536]{2,1,0:T(8,128)(2,1)}, bf16[2,32,1536]{2,1,0:T(8,128)(2,1)}, u32[]{:S(2)}, u32[]{:S(2)}) collective-permute-start(bf16[2,32,1536]{2,1,0:T(8,128)(2,1)} %fusion.63), channel_id=1, source_target_pairs={{0,16},{2,18},{4,20},{6,22},{8,24},{10,26},{12,28},{14,30},{16,0},... | collective-permute-start | bytes 589832 | tf_op jit(solution)/shard_map/ppermute | solution.py:190
  471.6 3.3 collective-permute-start.66
  478.3 46.6 %mixer_backward.1 = (bf16[32,64,256]{2,1,0:T(8,128)(2,1)S(1)}, f32[32,1,512]{2,1,0:T(1,128)S(1)}, f32[32,1,512]{2,1,0:T(1,128)S(1)}, f32[32,1,128]{2,1,0:T(1,128)S(1)}) custom-call(bf16[32,64,256]{2,1,0:T(8,128)(2,1)S(1)} %reshape.529.v_ref, bf16[32,64,256]{2,1,0:T(8,128)(2,1)S(1)} %reshape.538.dy_ref, f32[32,1,512]{2,1,0:T(1,128)S(1)} %copy-done.3, ...), custom_call_target="tpu_custom_call" | custom-call | tf_op jit(solution)/shard_map/mixer_backward/pallas_call | solution.py:174
  528.2 4.0 all-to-all-start.3
  539.6 8.7 %collective-permute-done.51 = bf16[32,1536]{1,0:T(8,128)(2,1)S(1)} collective-permute-done((bf16[32,1536]{1,0:T(8,128)(2,1)S(1)}, bf16[32,1536]{1,0:T(8,128)(2,1)S(1)}, u32[]{:S(2)}, u32[]{:S(2)}) %collective-permute-start.51) | collective-permute-done | bytes 98336 | tf_op jit(solution)/shard_map/ppermute | solution.py:190
  552.3 4.7 convolution_add_fusion
  566.0 6.2 fusion.19
  572.2 4.5 fusion.111
  578.6 5.1 multiply_reduce_fusion.1
  583.8 6.0 convert_reduce_fusion.3
  595.8 12.3 %collective-permute-done.39 = bf16[2,2,2,66,256]{3,4,1,0,2:T(8,128)(2,1)S(1)} collective-permute-done((bf16[2,2,2,66,256]{3,4,1,0,2:T(8,128)(2,1)S(1)}, bf16[2,2,2,66,256]{3,4,1,0,2:T(8,128)(2,1)S(1)}, u32[]{:S(2)}, u32[]{:S(2)}) %collective-permute-start.39) | collective-permute-done | bytes 270368 | tf_op jit(solution)/shard_map/ppermute | solution.py:190
  610.5 6.1 collective-permute-done.40
  617.8 7.0 %collective-permute-done.41 = bf16[2,66,256]{1,2,0:T(8,128)(2,1)S(1)} collective-permute-done((bf16[2,66,256]{1,2,0:T(8,128)(2,1)S(1)}, bf16[2,66,256]{1,2,0:T(8,128)(2,1)S(1)}, u32[]{:S(2)}, u32[]{:S(2)}) %collective-permute-start.41) | collective-permute-done | bytes 67616 | tf_op jit(solution)/shard_map/ppermute | solution.py:190
  625.5 3.6 collective-permute-done.42
  (587 shorter events, 206.1 us)
Async XLA Ops:
  2.6 20.9 %collective-permute-start.7 = (bf16[32,1536]{1,0:T(8,128)(2,1)S(1)}, bf16[32,1536]{1,0:T(8,128)(2,1)S(1)}, u32[]{:S(2)}, u32[]{:S(2)}) collective-permute-start(bf16[32,1536]{1,0:T(8,128)(2,1)S(1)} %select_n.720), channel_id=1, source_target_pairs={{0,1},{1,0},{2,3},{3,2},{4,5},{5,4},{6,7},{7,6},{8,9},{9,8},{10,11... | collective-permute-start | bytes 294920 | tf_op jit(solution)/shard_map/ppermute | solution.py:186
  8.7 108.3 %collective-permute-start = (bf16[1024,1024]{1,0:T(8,128)(2,1)}, bf16[1024,1024]{1,0:T(8,128)(2,1)S(1)}, u32[]{:S(2)}, u32[]{:S(2)}) collective-permute-start(bf16[1024,1024]{1,0:T(8,128)(2,1)} %param.16), channel_id=1, source_target_pairs={{0,1},{1,0},{2,3},{3,2},{4,5},{5,4},{6,7},{7,6},{8,9},{9,8},{10,11... | collective-permute-start | bytes 6291464 | tf_op jit(solution)/shard_map/ppermute | solution.py:186
  23.4 180.6 %collective-permute-start.36 = (bf16[1024,1024]{1,0:T(8,128)(2,1)}, bf16[1024,1024]{1,0:T(8,128)(2,1)}, u32[]{:S(2)}, u32[]{:S(2)}) collective-permute-start(bf16[1024,1024]{1,0:T(8,128)(2,1)} %param.17), channel_id=1, source_target_pairs={{0,1},{1,0},{2,3},{3,2},{4,5},{5,4},{6,7},{7,6},{8,9},{9,8},{10,11... | collective-permute-start | bytes 6291464 | tf_op jit(solution)/shard_map/ppermute | solution.py:186
  32.3 13.5 %collective-permute-start.19 = (bf16[2,16,1536]{2,1,0:T(8,128)(2,1)S(1)}, bf16[2,16,1536]{2,1,0:T(8,128)(2,1)S(1)}, u32[]{:S(2)}, u32[]{:S(2)}) collective-permute-start(bf16[2,16,1536]{2,1,0:T(8,128)(2,1)S(1)} %pad_maximum_fusion.28), channel_id=1, source_target_pairs={{0,16},{2,18},{4,20},{6,22},{8,24},{10,26},{12,28},{14,30},{16,0},... | collective-permute-start | bytes 294920 | tf_op jit(solution)/shard_map/ppermute | solution.py:190
  34.2 13.7 %collective-permute-start.24 = (bf16[2,16,1536]{2,1,0:T(8,128)(2,1)S(1)}, bf16[2,16,1536]{2,1,0:T(8,128)(2,1)S(1)}, u32[]{:S(2)}, u32[]{:S(2)}) collective-permute-start(bf16[2,16,1536]{2,1,0:T(8,128)(2,1)S(1)} %pad_maximum_fusion.29), channel_id=1, source_target_pairs={{0,16},{2,18},{4,20},{6,22},{8,24},{10,26},{12,28},{14,30},{16,0},... | collective-permute-start | bytes 294920 | tf_op jit(solution)/shard_map/ppermute | solution.py:190
  35.3 21.5 %collective-permute-start.28 = (bf16[2,48,1024]{2,1,0:T(8,128)(2,1)S(1)}, bf16[2,48,1024]{2,1,0:T(8,128)(2,1)S(1)}, u32[]{:S(2)}, u32[]{:S(2)}) collective-permute-start(bf16[2,48,1024]{2,1,0:T(8,128)(2,1)S(1)} %pad_maximum_fusion.23), channel_id=1, source_target_pairs={{0,16},{2,18},{4,20},{6,22},{8,24},{10,26},{12,28},{14,30},{16,0},... | collective-permute-start | bytes 589832 | tf_op jit(solution)/shard_map/ppermute | solution.py:190
  53.6 15.2 %collective-permute-start.13 = (bf16[2,32,1536]{2,1,0:T(8,128)(2,1)S(1)}, bf16[2,32,1536]{2,1,0:T(8,128)(2,1)S(1)}, u32[]{:S(2)}, u32[]{:S(2)}) collective-permute-start(bf16[2,32,1536]{2,1,0:T(8,128)(2,1)S(1)} %pad_maximum_fusion.20), channel_id=1, source_target_pairs={{0,16},{2,18},{4,20},{6,22},{8,24},{10,26},{12,28},{14,30},{16,0},... | collective-permute-start | bytes 589832 | tf_op jit(solution)/shard_map/ppermute | solution.py:190
  53.7 19.2 %collective-permute-start.9 = (bf16[2,32,1536]{2,1,0:T(8,128)(2,1)S(1)}, bf16[2,32,1536]{2,1,0:T(8,128)(2,1)S(1)}, u32[]{:S(2)}, u32[]{:S(2)}) collective-permute-start(bf16[2,32,1536]{2,1,0:T(8,128)(2,1)S(1)} %pad_maximum_fusion.19), channel_id=1, source_target_pairs={{0,16},{2,18},{4,20},{6,22},{8,24},{10,26},{12,28},{14,30},{16,0},... | collective-permute-start | bytes 589832 | tf_op jit(solution)/shard_map/ppermute | solution.py:190
  56.8 17.2 %collective-permute-start.20 = (bf16[2,2,16,1536]{3,2,0,1:T(8,128)(2,1)S(1)}, bf16[2,2,16,1536]{3,2,0,1:T(8,128)(2,1)S(1)}, u32[]{:S(2)}, u32[]{:S(2)}) collective-permute-start(bf16[2,2,16,1536]{3,2,0,1:T(8,128)(2,1)S(1)} %pad_maximum_fusion.21), channel_id=1, source_target_pairs={{0,2},{2,0},{4,6},{6,4},{8,10},{10,8},{12,14},{14,12},{16,18},{18,... | collective-permute-start | bytes 589832 | tf_op jit(solution)/shard_map/ppermute | solution.py:190
  68.9 18.0 %collective-permute-start.25 = (bf16[2,2,16,1536]{3,2,0,1:T(8,128)(2,1)S(1)}, bf16[2,2,16,1536]{3,2,0,1:T(8,128)(2,1)S(1)}, u32[]{:S(2)}, u32[]{:S(2)}) collective-permute-start(bf16[2,2,16,1536]{3,2,0,1:T(8,128)(2,1)S(1)} %pad_maximum_fusion.22), channel_id=1, source_target_pairs={{0,4},{2,6},{4,0},{6,2},{8,12},{10,14},{12,8},{14,10},{16,20},{18,... | collective-permute-start | bytes 589832 | tf_op jit(solution)/shard_map/ppermute | solution.py:190
  74.0 15.2 %collective-permute-start.6 = (bf16[2,2,2,67,256]{4,3,1,0,2:T(8,128)(2,1)S(1)}, bf16[2,2,2,67,256]{4,3,1,0,2:T(8,128)(2,1)S(1)}, u32[]{:S(2)}, u32[]{:S(2)}) collective-permute-start(bf16[2,2,2,67,256]{4,3,1,0,2:T(8,128)(2,1)S(1)} %pad_maximum_fusion.17), channel_id=1, source_target_pairs={{0,4},{2,6},{4,0},{6,2},{8,12},{10,14},{12,8},{14,10},{16,20},{18,... | collective-permute-start | bytes 823304 | tf_op jit(solution)/shard_map/ppermute | solution.py:190
  84.5 14.2 %collective-permute-start.29 = (bf16[2,2,48,1024]{3,2,1,0:T(8,128)(2,1)}, bf16[2,2,48,1024]{3,2,1,0:T(8,128)(2,1)}, u32[]{:S(2)}, u32[]{:S(2)}) collective-permute-start(bf16[2,2,48,1024]{3,2,1,0:T(8,128)(2,1)} %pad_maximum_fusion.14), channel_id=1, source_target_pairs={{0,2},{2,0},{4,6},{6,4},{8,10},{10,8},{12,14},{14,12},{16,18},{18,... | collective-permute-start | bytes 1179656 | tf_op jit(solution)/shard_map/ppermute | solution.py:190
  86.9 17.4 %collective-permute-start.10 = (bf16[2,2,32,1536]{3,2,1,0:T(8,128)(2,1)}, bf16[2,2,32,1536]{3,2,1,0:T(8,128)(2,1)}, u32[]{:S(2)}, u32[]{:S(2)}) collective-permute-start(bf16[2,2,32,1536]{3,2,1,0:T(8,128)(2,1)} %pad_maximum_fusion.10), channel_id=1, source_target_pairs={{0,2},{2,0},{4,6},{6,4},{8,10},{10,8},{12,14},{14,12},{16,18},{18,... | collective-permute-start | bytes 1179656 | tf_op jit(solution)/shard_map/ppermute | solution.py:190
  89.2 17.7 %collective-permute-start.14 = (bf16[2,2,32,1536]{3,2,1,0:T(8,128)(2,1)}, bf16[2,2,32,1536]{3,2,1,0:T(8,128)(2,1)}, u32[]{:S(2)}, u32[]{:S(2)}) collective-permute-start(bf16[2,2,32,1536]{3,2,1,0:T(8,128)(2,1)} %pad_maximum_fusion.11), channel_id=1, source_target_pairs={{0,4},{2,6},{4,0},{6,2},{8,12},{10,14},{12,8},{14,10},{16,20},{18,... | collective-permute-start | bytes 1179656 | tf_op jit(solution)/shard_map/ppermute | solution.py:190
  106.9 33.8 %collective-permute-start.33 = (bf16[2,2,48,1024]{3,2,1,0:T(8,128)(2,1)}, bf16[2,2,48,1024]{3,2,1,0:T(8,128)(2,1)}, u32[]{:S(2)}, u32[]{:S(2)}) collective-permute-start(bf16[2,2,48,1024]{3,2,1,0:T(8,128)(2,1)} %pad_maximum_fusion.15), channel_id=1, source_target_pairs={{0,4},{2,6},{4,0},{6,2},{8,12},{10,14},{12,8},{14,10},{16,20},{18,... | collective-permute-start | bytes 1179656 | tf_op jit(solution)/shard_map/ppermute | solution.py:190
  110.7 34.7 %collective-permute-start.30 = (bf16[2,2,2,48,1024]{4,3,1,0,2:T(8,128)(2,1)}, bf16[2,2,2,48,1024]{4,3,1,0,2:T(8,128)(2,1)}, u32[]{:S(2)}, u32[]{:S(2)}) collective-permute-start(bf16[2,2,2,48,1024]{4,3,1,0,2:T(8,128)(2,1)} %pad_maximum_fusion.6), channel_id=1, source_target_pairs={{0,4},{2,6},{4,0},{6,2},{8,12},{10,14},{12,8},{14,10},{16,20},{18,... | collective-permute-start | bytes 2359304 | tf_op jit(solution)/shard_map/ppermute | solution.py:190
  114.5 46.7 %collective-permute-start.11 = (bf16[2,2,2,32,1536]{4,3,1,0,2:T(8,128)(2,1)}, bf16[2,2,2,32,1536]{4,3,1,0,2:T(8,128)(2,1)}, u32[]{:S(2)}, u32[]{:S(2)}) collective-permute-start(bf16[2,2,2,32,1536]{4,3,1,0,2:T(8,128)(2,1)} %pad_maximum_fusion.4), channel_id=1, source_target_pairs={{0,4},{2,6},{4,0},{6,2},{8,12},{10,14},{12,8},{14,10},{16,20},{18,... | collective-permute-start | bytes 2359304 | tf_op jit(solution)/shard_map/ppermute | solution.py:190
  117.0 46.6 %collective-permute-start.15 = (bf16[2,2,2,32,1536]{4,3,1,0,2:T(8,128)(2,1)}, bf16[2,2,2,32,1536]{4,3,1,0,2:T(8,128)(2,1)}, u32[]{:S(2)}, u32[]{:S(2)}) collective-permute-start(bf16[2,2,2,32,1536]{4,3,1,0,2:T(8,128)(2,1)} %pad_maximum_fusion.5), channel_id=1, source_target_pairs={{0,2},{2,0},{4,6},{6,4},{8,10},{10,8},{12,14},{14,12},{16,18},{18,... | collective-permute-start | bytes 2359304 | tf_op jit(solution)/shard_map/ppermute | solution.py:190
  134.4 31.7 %all-to-all-start = ((bf16[8,32,2048]{2,1,0:T(8,128)(2,1)}), bf16[8,32,2048]{2,1,0:T(8,128)(2,1)S(1)}, u32[]{:S(2)}, u32[]{:S(2)}) async-start(bf16[8,32,2048]{2,1,0:T(8,128)(2,1)} %bitcast.416), calls=%async_computation | async-start | bytes 2097152 | tf_op jit(solution)/shard_map/all_to_all | solution.py:371
  143.5 56.7 %collective-permute-start.34 = (bf16[2,2,2,48,1024]{4,3,2,1,0:T(8,128)(2,1)}, bf16[2,2,2,48,1024]{4,3,2,1,0:T(8,128)(2,1)}, u32[]{:S(2)}, u32[]{:S(2)}) collective-permute-start(bf16[2,2,2,48,1024]{4,3,2,1,0:T(8,128)(2,1)} %pad_maximum_fusion.7), channel_id=1, source_target_pairs={{0,2},{2,0},{4,6},{6,4},{8,10},{10,8},{12,14},{14,12},{16,18},{18,... | collective-permute-start | bytes 2359304 | tf_op jit(solution)/shard_map/ppermute | solution.py:190
  191.9 16.7 %all-to-all-start.1 = ((bf16[8,32,2048]{2,1,0:T(8,128)(2,1)}), bf16[8,32,2048]{2,1,0:T(8,128)(2,1)}, u32[]{:S(2)}, u32[]{:S(2)}) async-start(bf16[8,32,2048]{2,1,0:T(8,128)(2,1)} %copy.219), calls=%async_computation.1 | async-start | bytes 2097152 | tf_op jit(solution)/shard_map/all_to_all | solution.py:371
  208.6 17.0 %collective-permute-start.17 = (bf16[256,2048]{1,0:T(8,128)(2,1)}, bf16[256,2048]{1,0:T(8,128)(2,1)S(1)}, u32[]{:S(2)}, u32[]{:S(2)}) collective-permute-start(bf16[256,2048]{1,0:T(8,128)(2,1)} %bitcast.45), channel_id=1, source_target_pairs={{0,1},{1,0},{2,3},{3,2},{4,5},{5,4},{6,7},{7,6},{8,9},{9,8},{10,11... | collective-permute-start | bytes 3145736 | tf_op jit(solution)/shard_map/ppermute | solution.py:186
  341.8 98.3 %collective-permute-start.37 = (bf16[256,2048]{1,0:T(8,128)(2,1)}, bf16[256,2048]{1,0:T(8,128)(2,1)}, u32[]{:S(2)}, u32[]{:S(2)}) collective-permute-start(bf16[256,2048]{1,0:T(8,128)(2,1)} %slice.365), channel_id=1, source_target_pairs={{0,1},{1,0},{2,3},{3,2},{4,5},{5,4},{6,7},{7,6},{8,9},{9,8},{10,11... | collective-permute-start | bytes 3145736 | tf_op jit(solution)/shard_map/ppermute | solution.py:186
  344.5 85.3 %collective-permute-start.63 = (bf16[2,2,2,48,1024]{4,3,1,0,2:T(8,128)(2,1)}, bf16[2,2,2,48,1024]{4,3,1,0,2:T(8,128)(2,1)}, u32[]{:S(2)}, u32[]{:S(2)}) collective-permute-start(bf16[2,2,2,48,1024]{4,3,1,0,2:T(8,128)(2,1)} %fusion.52), channel_id=1, source_target_pairs={{0,4},{2,6},{4,0},{6,2},{8,12},{10,14},{12,8},{14,10},{16,20},{18,... | collective-permute-start | bytes 2359304 | tf_op jit(solution)/shard_map/ppermute | solution.py:190
  345.9 86.3 %collective-permute-start.67 = (bf16[2,2,2,48,1024]{4,3,1,0,2:T(8,128)(2,1)S(1)}, bf16[2,2,2,48,1024]{4,3,1,0,2:T(8,128)(2,1)}, u32[]{:S(2)}, u32[]{:S(2)}) collective-permute-start(bf16[2,2,2,48,1024]{4,3,1,0,2:T(8,128)(2,1)S(1)} %fusion.53), channel_id=1, source_target_pairs={{0,2},{2,0},{4,6},{6,4},{8,10},{10,8},{12,14},{14,12},{16,18},{18,... | collective-permute-start | bytes 2359304 | tf_op jit(solution)/shard_map/ppermute | solution.py:190
  348.8 27.5 %collective-permute-start.54 = (bf16[2,2,2,16,1536]{4,3,0,2,1:T(8,128)(2,1)}, bf16[2,2,2,16,1536]{4,3,0,2,1:T(8,128)(2,1)}, u32[]{:S(2)}, u32[]{:S(2)}) collective-permute-start(bf16[2,2,2,16,1536]{4,3,0,2,1:T(8,128)(2,1)} %fusion.60), channel_id=1, source_target_pairs={{0,4},{2,6},{4,0},{6,2},{8,12},{10,14},{12,8},{14,10},{16,20},{18,... | collective-permute-start | bytes 1179656 | tf_op jit(solution)/shard_map/ppermute | solution.py:190
  350.9 22.8 %collective-permute-start.58 = (bf16[2,2,2,16,1536]{4,3,2,1,0:T(8,128)(2,1)}, bf16[2,2,2,16,1536]{4,3,2,1,0:T(8,128)(2,1)}, u32[]{:S(2)}, u32[]{:S(2)}) collective-permute-start(bf16[2,2,2,16,1536]{4,3,2,1,0:T(8,128)(2,1)} %fusion.57), channel_id=1, source_target_pairs={{0,2},{2,0},{4,6},{6,4},{8,10},{10,8},{12,14},{14,12},{16,18},{18,... | collective-permute-start | bytes 1179656 | tf_op jit(solution)/shard_map/ppermute | solution.py:190
  373.7 40.4 %collective-permute-start.48 = (bf16[2,2,2,32,1536]{4,3,1,0,2:T(8,128)(2,1)S(1)}, bf16[2,2,2,32,1536]{4,3,1,0,2:T(8,128)(2,1)S(1)}, u32[]{:S(2)}, u32[]{:S(2)}) collective-permute-start(bf16[2,2,2,32,1536]{4,3,1,0,2:T(8,128)(2,1)S(1)} %fusion.51), channel_id=1, source_target_pairs={{0,2},{2,0},{4,6},{6,4},{8,10},{10,8},{12,14},{14,12},{16,18},{18,... | collective-permute-start | bytes 2359304 | tf_op jit(solution)/shard_map/ppermute | solution.py:190
  382.1 14.2 %collective-permute-start.55 = (bf16[2,2,16,1536]{3,2,0,1:T(8,128)(2,1)S(1)}, bf16[2,2,16,1536]{3,2,0,1:T(8,128)(2,1)S(1)}, u32[]{:S(2)}, u32[]{:S(2)}) collective-permute-start(bf16[2,2,16,1536]{3,2,0,1:T(8,128)(2,1)S(1)} %fusion.64), channel_id=1, source_target_pairs={{0,2},{2,0},{4,6},{6,4},{8,10},{10,8},{12,14},{14,12},{16,18},{18,... | collective-permute-start | bytes 589832 | tf_op jit(solution)/shard_map/ppermute | solution.py:190
  413.5 14.5 %collective-permute-start.44 = (bf16[2,2,2,32,1536]{4,3,1,0,2:T(8,128)(2,1)S(1)}, bf16[2,2,2,32,1536]{4,3,1,0,2:T(8,128)(2,1)S(1)}, u32[]{:S(2)}, u32[]{:S(2)}) collective-permute-start(bf16[2,2,2,32,1536]{4,3,1,0,2:T(8,128)(2,1)S(1)} %fusion.50), channel_id=1, source_target_pairs={{0,4},{2,6},{4,0},{6,2},{8,12},{10,14},{12,8},{14,10},{16,20},{18,... | collective-permute-start | bytes 2359304 | tf_op jit(solution)/shard_map/ppermute | solution.py:190
  414.1 151.9 %collective-permute-start.35 = (bf16[1024,1024]{1,0:T(8,128)(2,1)}, bf16[1024,1024]{1,0:T(8,128)(2,1)}, u32[]{:S(2)}, u32[]{:S(2)}) collective-permute-start(bf16[1024,1024]{1,0:T(8,128)(2,1)} %slice.364), channel_id=1, source_target_pairs={{0,1},{1,0},{2,3},{3,2},{4,5},{5,4},{6,7},{7,6},{8,9},{9,8},{10,11... | collective-permute-start | bytes 6291464 | tf_op jit(solution)/shard_map/ppermute | solution.py:186
  432.2 17.1 %collective-permute-start.64 = (bf16[2,2,48,1024]{3,2,1,0:T(8,128)(2,1)}, bf16[2,2,48,1024]{3,2,1,0:T(8,128)(2,1)}, u32[]{:S(2)}, u32[]{:S(2)}) collective-permute-start(bf16[2,2,48,1024]{3,2,1,0:T(8,128)(2,1)} %fusion.58), channel_id=1, source_target_pairs={{0,2},{2,0},{4,6},{6,4},{8,10},{10,8},{12,14},{14,12},{16,18},{18,... | collective-permute-start | bytes 1179656 | tf_op jit(solution)/shard_map/ppermute | solution.py:190
  436.5 16.0 %collective-permute-start.68 = (bf16[2,2,48,1024]{3,2,1,0:T(8,128)(2,1)}, bf16[2,2,48,1024]{3,2,1,0:T(8,128)(2,1)}, u32[]{:S(2)}, u32[]{:S(2)}) collective-permute-start(bf16[2,2,48,1024]{3,2,1,0:T(8,128)(2,1)} %fusion.59), channel_id=1, source_target_pairs={{0,4},{2,6},{4,0},{6,2},{8,12},{10,14},{12,8},{14,10},{16,20},{18,... | collective-permute-start | bytes 1179656 | tf_op jit(solution)/shard_map/ppermute | solution.py:190
  437.0 23.7 %collective-permute-start.49 = (bf16[2,2,32,1536]{3,2,1,0:T(8,128)(2,1)}, bf16[2,2,32,1536]{3,2,1,0:T(8,128)(2,1)}, u32[]{:S(2)}, u32[]{:S(2)}) collective-permute-start(bf16[2,2,32,1536]{3,2,1,0:T(8,128)(2,1)} %fusion.56), channel_id=1, source_target_pairs={{0,4},{2,6},{4,0},{6,2},{8,12},{10,14},{12,8},{14,10},{16,20},{18,... | collective-permute-start | bytes 1179656 | tf_op jit(solution)/shard_map/ppermute | solution.py:190
  440.1 28.9 %collective-permute-start.45 = (bf16[2,2,32,1536]{3,2,1,0:T(8,128)(2,1)S(1)}, bf16[2,2,32,1536]{3,2,1,0:T(8,128)(2,1)S(1)}, u32[]{:S(2)}, u32[]{:S(2)}) collective-permute-start(bf16[2,2,32,1536]{3,2,1,0:T(8,128)(2,1)S(1)} %copy-done.83), channel_id=1, source_target_pairs={{0,2},{2,0},{4,6},{6,4},{8,10},{10,8},{12,14},{14,12},{16,18},{18,... | collective-permute-start | bytes 1179656 | tf_op jit(solution)/shard_map/ppermute | solution.py:190
  444.8 30.1 %all-to-all-start.2 = ((bf16[8,32,2048]{2,1,0:T(8,128)(2,1)}), bf16[8,32,2048]{2,1,0:T(8,128)(2,1)}, u32[]{:S(2)}, u32[]{:S(2)}) async-start(bf16[8,32,2048]{2,1,0:T(8,128)(2,1)} %bitcast.405), calls=%async_computation.2 | async-start | bytes 2097152 | tf_op jit(solution)/shard_map/all_to_all | solution.py:371
  450.8 19.3 %collective-permute-start.65 = (bf16[2,48,1024]{2,1,0:T(8,128)(2,1)S(1)}, bf16[2,48,1024]{2,1,0:T(8,128)(2,1)S(1)}, u32[]{:S(2)}, u32[]{:S(2)}) collective-permute-start(bf16[2,48,1024]{2,1,0:T(8,128)(2,1)S(1)} %fusion.66), channel_id=1, source_target_pairs={{0,16},{2,18},{4,20},{6,22},{8,24},{10,26},{12,28},{14,30},{16,0},... | collective-permute-start | bytes 589832 | tf_op jit(solution)/shard_map/ppermute | solution.py:190
  454.6 82.0 %collective-permute-start.69 = (bf16[2,48,1024]{2,1,0:T(8,128)(2,1)}, bf16[2,48,1024]{2,1,0:T(8,128)(2,1)}, u32[]{:S(2)}, u32[]{:S(2)}) collective-permute-start(bf16[2,48,1024]{2,1,0:T(8,128)(2,1)} %fusion.67), channel_id=1, source_target_pairs={{0,16},{2,18},{4,20},{6,22},{8,24},{10,26},{12,28},{14,30},{16,0},... | collective-permute-start | bytes 589832 | tf_op jit(solution)/shard_map/ppermute | solution.py:190
  462.6 69.5 %collective-permute-start.50 = (bf16[2,32,1536]{2,1,0:T(8,128)(2,1)}, bf16[2,32,1536]{2,1,0:T(8,128)(2,1)}, u32[]{:S(2)}, u32[]{:S(2)}) collective-permute-start(bf16[2,32,1536]{2,1,0:T(8,128)(2,1)} %fusion.63), channel_id=1, source_target_pairs={{0,16},{2,18},{4,20},{6,22},{8,24},{10,26},{12,28},{14,30},{16,0},... | collective-permute-start | bytes 589832 | tf_op jit(solution)/shard_map/ppermute | solution.py:190
  470.0 65.3 %collective-permute-start.46 = (bf16[2,32,1536]{2,1,0:T(8,128)(2,1)}, bf16[2,32,1536]{2,1,0:T(8,128)(2,1)}, u32[]{:S(2)}, u32[]{:S(2)}) collective-permute-start(bf16[2,32,1536]{2,1,0:T(8,128)(2,1)} %fusion.62), channel_id=1, source_target_pairs={{0,16},{2,18},{4,20},{6,22},{8,24},{10,26},{12,28},{14,30},{16,0},... | collective-permute-start | bytes 589832 | tf_op jit(solution)/shard_map/ppermute | solution.py:190
  471.6 90.4 %collective-permute-start.66 = (bf16[48,1024]{1,0:T(8,128)(2,1)}, bf16[48,1024]{1,0:T(8,128)(2,1)}, u32[]{:S(2)}, u32[]{:S(2)}) collective-permute-start(bf16[48,1024]{1,0:T(8,128)(2,1)} %fusion.75), channel_id=1, source_target_pairs={{0,8},{2,10},{4,12},{6,14},{8,0},{10,2},{12,4},{14,6},{16,24},{18,... | collective-permute-start | bytes 294920 | tf_op jit(solution)/shard_map/ppermute | solution.py:190
  528.2 21.3 %all-to-all-start.3 = ((bf16[8,32,2048]{2,1,0:T(8,128)(2,1)}), bf16[8,32,2048]{2,1,0:T(8,128)(2,1)S(1)}, u32[]{:S(2)}, u32[]{:S(2)}) async-start(bf16[8,32,2048]{2,1,0:T(8,128)(2,1)} %copy.200), calls=%async_computation.3 | async-start | bytes 2097152 | tf_op jit(solution)/shard_map/all_to_all | solution.py:371
  533.3 14.9 %collective-permute-start.51 = (bf16[32,1536]{1,0:T(8,128)(2,1)S(1)}, bf16[32,1536]{1,0:T(8,128)(2,1)S(1)}, u32[]{:S(2)}, u32[]{:S(2)}) collective-permute-start(bf16[32,1536]{1,0:T(8,128)(2,1)S(1)} %fusion.72), channel_id=1, source_target_pairs={{0,8},{2,10},{4,12},{6,14},{8,0},{10,2},{12,4},{14,6},{16,24},{18,... | collective-permute-start | bytes 294920 | tf_op jit(solution)/shard_map/ppermute | solution.py:190
  537.7 25.2 %collective-permute-start.70 = (bf16[48,1024]{1,0:T(8,128)(2,1)S(1)}, bf16[48,1024]{1,0:T(8,128)(2,1)S(1)}, u32[]{:S(2)}, u32[]{:S(2)}) collective-permute-start(bf16[48,1024]{1,0:T(8,128)(2,1)S(1)} %fusion.76), channel_id=1, source_target_pairs={{0,8},{2,10},{4,12},{6,14},{8,0},{10,2},{12,4},{14,6},{16,24},{18,... | collective-permute-start | bytes 294920 | tf_op jit(solution)/shard_map/ppermute | solution.py:190
  549.4 14.4 %collective-permute-start.52 = (f32[32,1536]{1,0:T(8,128)S(1)}, f32[32,1536]{1,0:T(8,128)S(1)}, u32[]{:S(2)}, u32[]{:S(2)}) collective-permute-start(f32[32,1536]{1,0:T(8,128)S(1)} %fusion.69), channel_id=1, source_target_pairs={{0,1},{1,0},{2,3},{3,2},{4,5},{5,4},{6,7},{7,6},{8,9},{9,8},{10,11... | collective-permute-start | bytes 589832 | tf_op jit(solution)/shard_map/ppermute | solution.py:186
  561.9 16.6 %collective-permute-start.38 = (bf16[1024,1024]{1,0:T(8,128)(2,1)}, bf16[1024,1024]{1,0:T(8,128)(2,1)}, u32[]{:S(2)}, u32[]{:S(2)}) collective-permute-start(bf16[1024,1024]{1,0:T(8,128)(2,1)} %slice.363), channel_id=1, source_target_pairs={{0,1},{1,0},{2,3},{3,2},{4,5},{5,4},{6,7},{7,6},{8,9},{9,8},{10,11... | collective-permute-start | bytes 6291464 | tf_op jit(solution)/shard_map/ppermute | solution.py:186
  593.8 14.4 %collective-permute-start.39 = (bf16[2,2,2,66,256]{3,4,1,0,2:T(8,128)(2,1)S(1)}, bf16[2,2,2,66,256]{3,4,1,0,2:T(8,128)(2,1)S(1)}, u32[]{:S(2)}, u32[]{:S(2)}) collective-permute-start(bf16[2,2,2,66,256]{3,4,1,0,2:T(8,128)(2,1)S(1)} %fusion.54), channel_id=1, source_target_pairs={{0,4},{2,6},{4,0},{6,2},{8,12},{10,14},{12,8},{14,10},{16,20},{18,... | collective-permute-start | bytes 811016 | tf_op jit(solution)/shard_map/ppermute | solution.py:190
  595.4 15.1 %collective-permute-start.71 = (f32[16,1152]{1,0:T(8,128)S(1)}, f32[16,1152]{1,0:T(8,128)S(1)}, u32[]{:S(2)}, u32[]{:S(2)}) collective-permute-start(f32[16,1152]{1,0:T(8,128)S(1)} %dynamic-slice_bitcast_fusion), channel_id=1, source_target_pairs={{0,16},{2,18},{4,20},{6,22},{8,24},{10,26},{12,28},{14,30},{16,0},... | collective-permute-start | bytes 221192 | tf_op jit(solution)/shard_map/ppermute | solution.py:190
  (134 other events, 1540.7 us)

commit v2 on v0

v2 whole, which is shorter than its diff:
```python
import functools

import jax
import jax.numpy as jnp
from jax import lax
from jax.experimental import pallas as pl
from jax.experimental.pallas import tpu as pltpu
from jax.sharding import PartitionSpec as P

SEQ = 16384
QBLK = 256
F32 = jnp.float32
BF = jnp.bfloat16
SWAP = [(0, 1), (1, 0)]


def mm(left, right, left_dim, right_dim):
    return lax.dot_general(
        left, right, (((left_dim,), (right_dim,)), ((), ())), preferred_element_type=F32
    )


def split(value):
    high = value.astype(BF)
    return high, (value - high.astype(F32)).astype(BF)


def iotas(rows, cols):
    return (
        lax.broadcasted_iota(jnp.int32, (rows, cols), 0),
        lax.broadcasted_iota(jnp.int32, (rows, cols), 1),
    )


def shift_rows(x, k, backward):
    n = x.shape[0]
    row = iotas(*x.shape)[0]
    if backward:
        return jnp.where(row < n - k, pltpu.roll(x, n - k, 0), 0.0)
    return jnp.where(row >= k, pltpu.roll(x, k, 0), 0.0)


def states(x, rate, group, backward):
    blocks = x.shape[0] // group
    order = list(range(blocks))[:: -1 if backward else 1]
    decay = jnp.exp(-rate * float(QBLK))
    local, state = {}, None
    for b in order:
        local[b] = state
        here = x[b * group : (b + 1) * group]
        state = here if state is None else state * decay + here
    k = 1
    while k < group:
        state = state + shift_rows(state, k, backward) * jnp.exp(-rate * float(QBLK * blocks * k))
        k *= 2
    carry = shift_rows(state, 1, backward)
    out = {}
    for step, b in enumerate(order):
        far = carry * jnp.exp(-rate * float(QBLK * step)) if step else carry
        out[b] = far if local[b] is None else far + local[b]
    return jnp.concatenate([out[b] for b in range(blocks)], axis=0)


def flip_matrix():
    i, j = iotas(QBLK, QBLK)
    return jnp.where(i + j == QBLK - 1, 1.0, 0.0).astype(BF)


def base_of(rate):
    return jnp.where(rate * float(QBLK) < 1.0, 1.0, 0.0)


def row_sums(x):
    return jnp.sum(x.astype(F32), axis=1, keepdims=True)


def through(rows, table, base):
    return mm(rows, table, 1, 0) + row_sums(rows) * base


def table_kernel(lr_ref, co_ref, d_ref, dt_ref, t_ref):
    i, j = iotas(QBLK, QBLK)
    for c in range(lr_ref.shape[0]):
        rate, coeff = jnp.exp(lr_ref[c]), co_ref[c]
        row = lax.broadcasted_iota(jnp.int32, (8, rate.shape[1]), 0).astype(F32)
        table = jnp.exp(-rate * row)
        step = 8
        while step < QBLK:
            table = jnp.concatenate([table, table * jnp.exp(-rate * float(step))], axis=0)
            step *= 2
        lowered = table - base_of(rate)
        d_ref[c] = lowered.astype(BF)
        turned = lowered.T
        dt_ref[c] = turned.astype(BF)
        high, low = split(jnp.broadcast_to(coeff, (8, coeff.shape[1])))
        t_high, t_low = split(turned)
        kern = (
            mm(high, t_high, 1, 0) + mm(low, t_high, 1, 0) + mm(high, t_low, 1, 0)
        )[0:1] + row_sums(coeff * base_of(rate))
        rolled = pltpu.roll(jnp.broadcast_to(kern, (QBLK, QBLK)), 0, 1, stride=1, stride_axis=0)
        t_ref[c] = jnp.where(j >= i, rolled, 0.0).astype(BF)


def far_rows(entering, scale, turned, base):
    rows = entering.shape[0]
    scaled = entering * scale
    both = mm(jnp.concatenate(split(scaled), axis=0), turned, 1, 0)
    return both[:rows] + both[rows:] + row_sums(scaled * base)


def lanes_of(b, turn, total):
    start = b * QBLK + turn * (total // 2)
    start = jnp.where(start >= total, start - total, start)
    return pl.ds(pl.multiple_of(start, QBLK), QBLK)


def take_rows(x_ref, rows_ref, turn):
    group, _, total = x_ref.shape
    for b in range(0, total // QBLK, 2):
        pair = [
            jnp.swapaxes(x_ref[:, :, lanes_of(b + k, turn, total)].astype(F32), 0, 1)
            for k in range(2)
        ]
        rows_ref[:, b * group : (b + 2) * group, :] = jnp.concatenate(pair, axis=1).astype(BF)


def give_rows(rows_ref, x_ref, turn):
    group, _, total = x_ref.shape
    for b in range(0, total // QBLK, 2):
        pair = rows_ref[:, b * group : (b + 2) * group, :].astype(F32)
        for k in range(2):
            x_ref[:, :, lanes_of(b + k, turn, total)] = jnp.swapaxes(
                pair[:, k * group : (k + 1) * group], 0, 1
            ).astype(BF)


def forward_kernel(turn_ref, v_ref, d_ref, dt_ref, t_ref, lr_ref, co_ref, sk_ref, y_ref, en_ref, rows_ref, back_ref):
    per, group, turn = d_ref.shape[0], v_ref.shape[0], turn_ref[0]
    part, parts = pl.program_id(1), pl.num_programs(1)
    count = rows_ref.shape[1]

    @pl.when(part == 0)
    def _():
        take_rows(v_ref, rows_ref, turn)

    mine = rows_ref[pl.ds(part * per, per)]
    flipped = mm(mine.reshape(per * count, QBLK), flip_matrix(), 1, 0).astype(BF)
    for c in range(per):
        v = mine[c]
        rate = jnp.exp(lr_ref[c])
        base = base_of(rate)
        ends = through(flipped[c * count : (c + 1) * count], d_ref[c], base)
        entering = states(ends, rate, group, False)
        en_ref[c] = entering
        far = far_rows(entering, co_ref[c] * jnp.exp(-rate), dt_ref[c], base)
        back_ref[part * per + c] = (
            far + mm(v, t_ref[c], 1, 0) + sk_ref[c][:, :1] * v.astype(F32)
        ).astype(BF)

    @pl.when(part == parts - 1)
    def _():
        give_rows(back_ref, y_ref, turn)


def backward_kernel(
    turn_ref, v_ref, dy_ref, en_ref, d_ref, dt_ref, t_ref, lr_ref, co_ref, sk_ref,
    dv_ref, gr_ref, gc_ref, gs_ref, v_rows_ref, dy_rows_ref, back_ref,
):
    per, group, turn = d_ref.shape[0], v_ref.shape[0], turn_ref[0]
    part, parts = pl.program_id(1), pl.num_programs(1)
    count = v_rows_ref.shape[1]
    rows = per * count

    @pl.when(part == 0)
    def _():
        take_rows(v_ref, v_rows_ref, turn)
        take_rows(dy_ref, dy_rows_ref, turn)

    flip = flip_matrix()
    v_all = v_rows_ref[pl.ds(part * per, per)].reshape(rows, QBLK)
    dy_all = dy_rows_ref[pl.ds(part * per, per)].reshape(rows, QBLK)
    flipped = mm(jnp.concatenate([v_all, dy_all], axis=0), flip, 1, 0)
    lane = lax.broadcasted_iota(jnp.int32, (rows, QBLK), 1).astype(F32)
    v_lag = (flipped[:rows] * lane).astype(BF)
    dy_lag = (dy_all.astype(F32) * lane).astype(BF)
    flipped = flipped.astype(BF)
    i, j = iotas(QBLK, QBLK)
    lag = lax.broadcasted_iota(jnp.int32, (1, QBLK), 1).astype(F32)
    back = []
    for c in range(per):
        here = slice(c * count, (c + 1) * count)
        dy = dy_all[here]
        v_flip, dy_flip = flipped[here], flipped[rows + c * count : rows + (c + 1) * count]
        rate, coeff = jnp.exp(lr_ref[c]), co_ref[c]
        base = base_of(rate)
        pairs = pltpu.roll(mm(v_flip, dy, 0, 0), 1, 1, stride=1, stride_axis=0)
        near = jnp.sum(jnp.where(j <= i, pairs, 0.0), axis=0, keepdims=True)
        near_rows = jnp.concatenate(
            split(
                jnp.concatenate(
                    [jnp.broadcast_to(near, (8, QBLK)), jnp.broadcast_to(near * lag, (8, QBLK))],
                    axis=0,
                )
            ),
            axis=0,
        )
        sums = through(
            jnp.concatenate([dy, dy_lag[here], v_lag[here], near_rows], axis=0), d_ref[c], base
        )
        starts, starts_lag, ends_lag = (sums[k * count : (k + 1) * count] for k in range(3))
        inner = sums[3 * count : 3 * count + 16] + sums[3 * count + 16 :]
        leaving = states(starts, rate, group, True)
        entering = en_ref[c]
        one = jnp.exp(-rate)
        far = far_rows(leaving, coeff * one, dt_ref[c], base)
        back.append(
            (
                far + mm(dy_flip, t_ref[c], 1, 0) + sk_ref[c][:, :1] * dy_flip.astype(F32)
            ).astype(BF)
        )
        whole = jnp.exp(-rate * float(QBLK))
        outer = jnp.sum(entering * starts, axis=0, keepdims=True)
        moment = jnp.sum(
            ends_lag * leaving + entering * (starts_lag + (float(QBLK) * whole) * leaving),
            axis=0,
            keepdims=True,
        )
        gc_ref[c] = inner[0:1] + one * outer
        gr_ref[c] = -(coeff * rate) * (inner[8:9] + one * (moment + outer))
        gs_ref[c] = jnp.broadcast_to(near[:, :1], (1, 128))
    turned = mm(jnp.concatenate(back, axis=0), flip, 1, 0).astype(BF)
    back_ref[pl.ds(part * per, per)] = turned.reshape(per, count, QBLK)

    @pl.when(part == parts - 1)
    def _():
        give_rows(back_ref, dv_ref, turn)


def mixer_tables(log_rate, coeff):
    chans, _, n = log_rate.shape
    per = 4

    def spec(rows, cols):
        return pl.BlockSpec((per, rows, cols), lambda i: (i, 0, 0))

    shapes = [(QBLK, n), (n, QBLK), (QBLK, QBLK)]
    return pl.pallas_call(
        table_kernel,
        grid=(chans // per,),
        in_specs=[spec(1, n)] * 2,
        out_specs=[spec(*shape) for shape in shapes],
        out_shape=[jax.ShapeDtypeStruct((chans,) + shape, BF) for shape in shapes],
        compiler_params=pltpu.CompilerParams(vmem_limit_bytes=32 * 2**20),
        name="mixer_tables",
    )(log_rate, coeff)


def mixer_call(kernel, turn, tokens_in, by_channel, outs, name):
    group, chans, total = tokens_in[0].shape
    tall, per = 16, 8
    parts = tall // per
    count = group * (total // QBLK)

    def spec(shape):
        return pl.BlockSpec((per,) + tuple(shape[1:]), lambda i, j, *_: (i * parts + j, 0, 0))

    wide = pl.BlockSpec((group, tall, total), lambda i, j, *_: (0, i, 0))
    return pl.pallas_call(
        kernel,
        grid_spec=pltpu.PrefetchScalarGridSpec(
            num_scalar_prefetch=1,
            grid=(chans // tall, parts),
            in_specs=[wide] * len(tokens_in) + [spec(x.shape) for x in by_channel],
            out_specs=[wide] + [spec(shape) for shape, _ in outs],
            scratch_shapes=[pltpu.VMEM((tall, count, QBLK), BF)] * (len(tokens_in) + 1),
        ),
        out_shape=[jax.ShapeDtypeStruct((group, chans, total), BF)]
        + [jax.ShapeDtypeStruct(shape, kind) for shape, kind in outs],
        compiler_params=pltpu.CompilerParams(vmem_limit_bytes=40 * 2**20),
        name=name,
    )(turn, *tokens_in, *by_channel)


def mixer_forward(turn, v, tables, params):
    group, chans, total = v.shape
    n = params[0].shape[2]
    states_of = (chans, group * (total // QBLK), n)
    return mixer_call(
        forward_kernel, turn, [v], [*tables, *params], [(states_of, F32)], "mixer_forward"
    )


def mixer_backward(turn, v, dy, entering, tables, params):
    chans, n = v.shape[1], params[0].shape[2]
    return mixer_call(
        backward_kernel,
        turn,
        [v, dy],
        [entering, *tables, *params],
        [((chans, 1, n), F32), ((chans, 1, n), F32), ((chans, 1, 128), F32)],
        "mixer_backward",
    )


TILE = 512


def call(kernel, grid, core, ins, outs, name, room=24):
    return pl.pallas_call(
        kernel,
        grid_spec=pltpu.PrefetchScalarGridSpec(
            num_scalar_prefetch=1,
            grid=(grid,),
            in_specs=[
                pl.BlockSpec(block, index, pipeline_mode=None if index in MOVING else pl.Buffered(1))
                for _, block, index in ins
            ],
            out_specs=[pl.BlockSpec(block, index) for _, _, block, index in outs],
        ),
        out_shape=[jax.ShapeDtypeStruct(shape, kind) for shape, kind, _, _ in outs],
        compiler_params=pltpu.CompilerParams(vmem_limit_bytes=room * 2**20),
        cost_estimate=pl.CostEstimate(flops=0, bytes_accessed=0, transcendentals=0),
        name=name,
    )(core, *[array for array, _, _ in ins])


def row_tile(m, _):
    return (m, 0)


def col_tile(m, _):
    return (0, m)


def turned_tile(m, _):
    half = pl.num_programs(0) // 2
    return (0, jnp.where(m < half, m + half, m - half))


def fixed(m, _):
    return (0, 0)


MOVING = (row_tile, col_tile, turned_tile)


def first_rows(m, _):
    return (jnp.minimum(m, pl.num_programs(0) // 2 - 1), 0)


def last_rows(m, _):
    return (jnp.maximum(m - pl.num_programs(0) // 2, 0), 0)


def strips_of(start, stop, strip):
    while start < stop:
        k = start // strip
        end = min(stop, (k + 1) * strip)
        yield k, slice(start - k * strip, end - k * strip)
        start = end


def strip_columns(ref, strips, start, stop, order):
    rows = ref.shape[2] // strips
    return jnp.concatenate(
        [
            jnp.concatenate(
                [
                    ref[chip, core, k * rows : (k + 1) * rows, lanes]
                    for chip in order
                    for core in range(ref.shape[1])
                ],
                axis=0,
            )
            for k, lanes in strips_of(start, stop, ref.shape[3])
        ],
        axis=1,
    )


def strip_rows(ref, strips, start, stop):
    rows = ref.shape[2] // strips
    return jnp.concatenate(
        [
            jnp.concatenate(
                [
                    ref[chip, 0, k * rows + part.start : k * rows + part.stop, :]
                    for chip, part in strips_of(start, stop, rows)
                ],
                axis=0,
            )
            for k in range(strips)
        ],
        axis=1,
    )


def col_sum(x):
    return jnp.sum(x.astype(F32), axis=0, keepdims=True)


def hat_of(x):
    x = x.astype(F32)
    centered = x - jnp.mean(x, axis=-1, keepdims=True)
    inv_std = lax.rsqrt(jnp.mean(centered * centered, axis=-1, keepdims=True) + 1e-05)
    return centered * inv_std, inv_std


def slope_and_gelu(h):
    phi = 0.5 + 0.5 * lax.erf(h * 0.7071067811865476)
    return h * phi, phi + h * jnp.exp(-0.5 * h * h) * 0.3989422804014327


def norm_kernel(
    _, tok_ref, cot_ref, live_ref, gain_ref, bias_ref, w_ref, b_ref, n_ref, g_ref, v_ref, s_ref, sum_ref
):
    m = pl.program_id(0)

    @pl.when(m == 0)
    def _():
        sum_ref[...] = jnp.zeros_like(sum_ref)

    hat, _ = hat_of(tok_ref[...])
    normed = (hat * gain_ref[...] + bias_ref[...]).astype(BF)
    n_ref[...] = normed
    g = jnp.where(live_ref[...][:, :1] > 0.0, cot_ref[...], jnp.zeros((), BF))
    g_ref[...] = g

    @pl.when(m < pl.num_programs(0) // 2)
    def _():
        sum_ref[...] += col_sum(g)

    v, s = slope_and_gelu(mm(w_ref[...], normed, 1, 1) + b_ref[...][:, :1])
    v_ref[...] = v.astype(BF)
    s_ref[...] = s.astype(BF)


def norm_call(core, tok, cot, live, gain, bias, w_turned, b):
    tokens, width = tok.shape
    chans = w_turned.shape[0]
    rows, cols = (TILE, width), (chans, TILE)
    return call(
        norm_kernel,
        tokens // TILE,
        core,
        [
            (tok, rows, row_tile),
            (cot, rows, row_tile),
            (live, (TILE, 128), row_tile),
            (gain, (1, width), fixed),
            (bias, (1, width), fixed),
            (w_turned, (chans, width), fixed),
            (b, (chans, 128), fixed),
        ],
        [((tokens, width), BF, rows, row_tile)] * 2
        + [((chans, tokens), BF, cols, col_tile)] * 2
        + [((1, width), F32, (1, width), fixed)],
        "norm",
    )


def early_kernel(
    _, x_ref, g_ref, b1_ref, w1_ref, w4_ref, w3m_ref, w3o_ref,
    u_ref, dzs_ref, dgate_ref, mine_ref, other_ref, sum_ref, *, order,
):
    total = u_ref.shape[1]
    cols, strips = 384, total // w1_ref.shape[3]
    chips = range(w1_ref.shape[0])
    e_strips = g_ref.shape[1] // w4_ref.shape[3]

    @pl.when(pl.program_id(0) == 0)
    def _():
        sum_ref[...] = jnp.zeros_like(sum_ref)

    for n in range(total // cols):
        at = slice(n * cols, (n + 1) * cols)
        w1 = strip_columns(w1_ref, strips, at.start, at.stop, chips)
        u, s = slope_and_gelu(mm(x_ref[...], w1, 1, 0) + b1_ref[:, at])
        dz = mm(g_ref[...], strip_rows(w4_ref, e_strips, at.start, at.stop), 1, 1)
        dgate = (dz * u).astype(BF)
        u_ref[:, at] = u.astype(BF)
        dzs_ref[:, at] = (dz * s).astype(BF)
        dgate_ref[:, at] = dgate
        sum_ref[:, at] += col_sum(dgate)
    mine_ref[...] = mm(strip_columns(w3m_ref, strips, 0, total, order), dgate_ref[...], 1, 1)
    other = mm(strip_columns(w3o_ref, strips, 0, total, order), dgate_ref[...], 1, 1)
    other_ref[...] = other.astype(BF)


def early_call(core, x, g, b1, weights, order):
    tokens, width = x.shape
    cols = b1.shape[1]
    chans = weights[2][1][2] * weights[2][1][3] * len(order) // cols
    wide, tall = (TILE, cols), (chans, TILE)
    return call(
        functools.partial(early_kernel, order=order),
        tokens // TILE,
        core,
        [
            (x, (TILE, width), row_tile),
            (g, (TILE, width), row_tile),
            (b1, (1, cols), fixed),
            *weights,
        ],
        [((tokens, cols), BF, wide, row_tile)] * 3
        + [
            ((chans, tokens), F32, tall, col_tile),
            ((chans, tokens), BF, tall, turned_tile),
            ((1, cols), F32, (1, cols), fixed),
        ],
        "early",
        40,
    )


def late_kernel(
    _, ym_ref, yo_ref, b3_ref, u_ref, dzs_ref, w1_ref, w4_ref, w3m_ref, w3o_ref,
    z_ref, dh_ref, om_ref, oo_ref, p_ref, sum_ref, *, order,
):
    m, total = pl.program_id(0), u_ref.shape[1]
    cols, strips = 256, total // w1_ref.shape[3]
    chips = range(w1_ref.shape[0])
    e_strips = om_ref.shape[1] // w4_ref.shape[3]

    @pl.when(m == 0)
    def _():
        sum_ref[...] = jnp.zeros_like(sum_ref)

    y = jnp.concatenate([ym_ref[...], yo_ref[...]], axis=0).T
    for n in range(total // cols):
        at = slice(n * cols, (n + 1) * cols)
        w3 = jnp.concatenate(
            [strip_columns(ref, strips, at.start, at.stop, order) for ref in (w3m_ref, w3o_ref)],
            axis=0,
        )
        gate = mm(y, w3, 1, 0) + b3_ref[:, at]
        z_ref[:, at] = (u_ref[:, at].astype(F32) * gate).astype(BF)
        dh = (dzs_ref[:, at].astype(F32) * gate).astype(BF)
        dh_ref[:, at] = dh
        sum_ref[:, at] += col_sum(dh)
    p_ref[...] = mm(dh_ref[...], strip_columns(w1_ref, strips, 0, total, chips), 1, 1).astype(BF)
    out = mm(z_ref[...], strip_rows(w4_ref, e_strips, 0, total), 1, 0)

    @pl.when(m < pl.num_programs(0) // 2)
    def _():
        om_ref[...] = out

    @pl.when(m >= pl.num_programs(0) // 2)
    def _():
        oo_ref[...] = out.astype(BF)


def late_call(core, y_mine, y_other, b3, u, dzs, width, weights, order):
    tokens, cols = u.shape
    wide, tall = (TILE, cols), (y_mine.shape[0], TILE)
    rows = (TILE, width)
    return call(
        functools.partial(late_kernel, order=order),
        tokens // TILE,
        core,
        [
            (y_mine, tall, col_tile),
            (y_other, tall, turned_tile),
            (b3, (1, cols), fixed),
            (u, wide, row_tile),
            (dzs, wide, row_tile),
            *weights,
        ],
        [
            ((tokens, cols), BF, wide, row_tile),
            ((tokens, cols), BF, wide, row_tile),
            ((tokens // 2, width), F32, rows, first_rows),
            ((tokens // 2, width), BF, rows, last_rows),
            ((tokens, width), BF, rows, row_tile),
            ((1, cols), F32, (1, cols), fixed),
        ],
        "late",
        40,
    )


def tail_kernel(_, dv_ref, s_ref, w_ref, p_ref, tok_ref, dh_ref, pm_ref, po_ref, gain_ref, bias_ref, sum_ref):
    m = pl.program_id(0)

    @pl.when(m == 0)
    def _():
        gain_ref[...] = jnp.zeros_like(gain_ref)
        bias_ref[...] = jnp.zeros_like(bias_ref)
        sum_ref[...] = jnp.zeros_like(sum_ref)

    dh = (dv_ref[...].astype(F32) * s_ref[...].astype(F32)).astype(BF)
    dh_ref[...] = dh
    for k in range(dh.shape[1] // 128):
        sum_ref[...] += dh[:, k * 128 : (k + 1) * 128].astype(F32)
    p = p_ref[...].astype(F32) + mm(dh.T, w_ref[...], 1, 0)
    hat, _ = hat_of(tok_ref[...])
    gain_ref[...] += col_sum(p * hat)
    bias_ref[...] += col_sum(p)

    @pl.when(m < pl.num_programs(0) // 2)
    def _():
        pm_ref[...] = p

    @pl.when(m >= pl.num_programs(0) // 2)
    def _():
        po_ref[...] = p.astype(BF)


def tail_call(core, dv, slope, w_turned, p, tok):
    chans, tokens = dv.shape
    width = p.shape[1]
    rows, cols = (TILE, width), (chans, TILE)
    return call(
        tail_kernel,
        tokens // TILE,
        core,
        [
            (dv, cols, col_tile),
            (slope, cols, col_tile),
            (w_turned, (chans, width), fixed),
            (p, rows, row_tile),
            (tok, rows, row_tile),
        ],
        [
            ((chans, tokens), BF, cols, col_tile),
            ((tokens // 2, width), F32, rows, first_rows),
            ((tokens // 2, width), BF, rows, last_rows),
            ((1, width), F32, (1, width), fixed),
            ((1, width), F32, (1, width), fixed),
            ((chans, 128), F32, (chans, 128), fixed),
        ],
        "tail",
    )


def input_kernel(_, mine_ref, got_ref, tok_ref, g_ref, gain_ref, out_ref):
    hat, inv_std = hat_of(tok_ref[...])
    grad = (mine_ref[...] + got_ref[...].astype(F32)) * gain_ref[...]
    out_ref[...] = (
        g_ref[...].astype(F32)
        + inv_std
        * (
            grad
            - jnp.mean(grad, axis=-1, keepdims=True)
            - hat * jnp.mean(grad * hat, axis=-1, keepdims=True)
        )
    ).astype(BF)


def input_call(core, mine, got, tok, g, gain):
    tokens, width = mine.shape
    rows = (256, width)
    return call(
        input_kernel,
        tokens // 256,
        core,
        [(x, rows, row_tile) for x in (mine, got, tok, g)] + [(gain, (1, width), fixed)],
        [((tokens, width), BF, rows, row_tile)],
        "input_grad",
    )[0]

def keep_and_send(bit_ref, out, runs, keep_ref, send_ref):
    low, high = (
        jnp.concatenate(
            [out[k * runs : (k + 1) * runs] for k in range(half, out.shape[0] // runs, 2)], axis=0
        )
        for half in range(2)
    )
    one = bit_ref[0] == 1

    @pl.when(one)
    def _():
        keep_ref[...] = high
        send_ref[...] = low.astype(BF)

    @pl.when(jnp.logical_not(one))
    def _():
        keep_ref[...] = low
        send_ref[...] = high.astype(BF)


def grad_kernel(bit_ref, a_ref, b_ref, keep_ref, send_ref, *, runs):
    keep_and_send(bit_ref, mm(a_ref[...], b_ref[...], 0, 0), runs, keep_ref, send_ref)


def grad_call(bit, a, b, runs, tile, name):
    rows, cols = a.shape[1], b.shape[1]
    half = (tile // 2, cols)
    return call(
        functools.partial(grad_kernel, runs=runs),
        rows // tile,
        bit,
        [(a, (a.shape[0], tile), col_tile), (b, b.shape, fixed)],
        [((rows // 2, cols), F32, half, row_tile), ((rows // 2, cols), BF, half, row_tile)],
        name,
        32,
    )


def mixed_grad_kernel(bit_ref, ym_ref, yo_ref, b_ref, keep_ref, send_ref, *, runs):
    half = b_ref.shape[0] // 2
    out = jnp.concatenate(
        [
            mm(ym_ref[...], b_ref[...], 1, 0),
            mm(yo_ref[:, half:], b_ref[:half], 1, 0) + mm(yo_ref[:, :half], b_ref[half:], 1, 0),
        ],
        axis=0,
    )
    keep_and_send(bit_ref, out, runs, keep_ref, send_ref)


def mixed_grad_call(bit, y_mine, y_other, b, runs, name):
    rows, cols, tile = 2 * y_mine.shape[0], b.shape[1], 512
    half = (rows // 2, tile)
    return call(
        functools.partial(mixed_grad_kernel, runs=runs),
        cols // tile,
        bit,
        [(y_mine, y_mine.shape, fixed), (y_other, y_other.shape, fixed), (b, (b.shape[0], tile), col_tile)],
        [((rows // 2, cols), F32, half, col_tile), ((rows // 2, cols), BF, half, col_tile)],
        name,
        32,
    )


def after(x, *others):
    return lax.optimization_barrier((x,) + others)[0]


def swap_cores(x):
    return lax.ppermute(x, "fsdp", SWAP)


def across(x, size, bit):
    return lax.ppermute(x, "dp", [(i, i ^ (1 << bit)) for i in range(size)])


def bit_of(bit):
    return (lax.axis_index("dp") >> bit) & 1


def gather_bits(x, size, order, layout):
    have = []
    for bit in order:
        other = across(x, size, bit)
        mine = bit_of(bit) == 1
        have = [b for b in layout if b in have or b == bit]
        x = jnp.stack(
            [jnp.where(mine, other, x), jnp.where(mine, x, other)], axis=have.index(bit)
        )
    return x


def scatter_bits(x, size, order, layout, send_type):
    have = list(layout)
    for bit in order:
        axis = have.index(bit)
        mine = bit_of(bit)
        theirs = lax.dynamic_index_in_dim(x, 1 - mine, axis, keepdims=False)
        kept = lax.dynamic_index_in_dim(x, mine, axis, keepdims=False)
        x = kept.astype(F32) + across(theirs.astype(send_type), size, bit).astype(F32)
        have.remove(bit)
    return x


def per_device(
    size,
    tokens,
    cotangent,
    lengths,
    norm_gain,
    norm_bias,
    w_one,
    b_one,
    w_two,
    b_two,
    w_three,
    b_three,
    w_four,
    b_four,
    log_rate,
    ssm_coeff,
    ssm_skip,
):
    bits = size.bit_length() - 1
    tok_dev, width = tokens.shape
    rows_e, rows_f, rows_h = w_one.shape[0], w_four.shape[0], w_three.shape[0]
    f_half, h_half = size * rows_f, size * rows_h
    buckets = lengths.shape[0]
    group = size // buckets
    group_bits = group.bit_length() - 1
    chans = buckets * rows_h
    tok_chip = 2 * tok_dev
    per_dev = tok_dev // QBLK
    nstate = log_rate.shape[1]
    natural = list(range(bits))[::-1]
    by_owner = natural[bits - group_bits :] + natural[: bits - group_bits]
    top = natural[: bits - group_bits]
    order_a = list(range(2, bits)) + [0, 1]
    order_b = list(range(2, bits)) + [1, 0]
    core = lax.axis_index("fsdp")
    first = core == 0
    chip = lax.axis_index("dp")
    core_at = jnp.reshape(core, (1,)).astype(jnp.int32)
    everyone = ("dp", "fsdp")

    def natural_pair(mine, other, axis=0):
        return jnp.stack(
            [jnp.where(first, mine, other), jnp.where(first, other, mine)], axis=axis
        )

    def mine_other(parts, axis):
        a = lax.index_in_dim(parts, 0, axis, keepdims=False)
        b = lax.index_in_dim(parts, 1, axis, keepdims=False)
        return jnp.where(first, a, b), jnp.where(first, b, a)

    tok_pair = jnp.concatenate([tokens, swap_cores(tokens)], axis=0)
    cot_pair = jnp.concatenate([cotangent, swap_cores(cotangent)], axis=0)

    two_parts = jnp.moveaxis(
        w_two.reshape(rows_e, buckets, group, 2, rows_h), (3, 2, 1), (0, 2, 3)
    ).reshape(2, rows_e, h_half)
    vec = jnp.concatenate([norm_gain, norm_bias, b_four, b_one, b_three, b_two])
    vec_len = vec.shape[0]
    vec_rows = -(-vec_len // h_half)
    vec = jnp.pad(vec, (0, vec_rows * h_half - vec_len)).reshape(1, vec_rows, h_half)
    small = jnp.concatenate(
        [two_parts, jnp.broadcast_to(vec, (2, vec_rows, h_half))], axis=1
    )
    small = jnp.broadcast_to(small[None], (size, 2) + small.shape[1:])
    small = lax.all_to_all(
        small.reshape((2 * size,) + small.shape[2:]), everyone, split_axis=0, concat_axis=0
    )
    two_turned = small[:, :rows_e].reshape(width, h_half).T
    vecs = small[:, rows_e:].reshape(2 * size, -1)[:, :vec_len].astype(F32)
    gain_f = vecs[:, :rows_e].reshape(1, width)
    nbias_f = vecs[:, rows_e : 2 * rows_e].reshape(1, width)
    bfour_f = vecs[:, 2 * rows_e : 3 * rows_e].reshape(1, width)
    own_vecs, _ = mine_other(vecs.reshape(size, 2, vec_len)[:, :, 3 * rows_e :], 1)
    bone_f = own_vecs[:, :rows_f].reshape(1, f_half)
    bthree_f = own_vecs[:, rows_f : 2 * rows_f].reshape(1, f_half)
    btwo_f = (
        own_vecs[:, 2 * rows_f :].reshape(buckets, group, rows_h).swapaxes(0, 1).reshape(h_half, 1)
    )

    strip = 512
    f_strips, e_strips = f_half // strip, width // strip

    def by_half(x):
        rows = x.shape[0]
        parts = jnp.moveaxis(x.reshape(rows, size, 2, rows_f), 2, 0).reshape(2, rows, f_half)
        parts = jnp.moveaxis(parts.reshape(2, rows, f_strips, strip), 2, 1)
        return parts.reshape(2 * f_strips * rows, strip)

    packed = jnp.concatenate(
        [w_four[:, k * strip : (k + 1) * strip] for k in range(e_strips)]
        + [by_half(w_one), by_half(w_three)],
        axis=0,
    )
    gathered = lax.all_gather(packed, everyone, axis=0)
    four_end = e_strips * rows_f
    one_end = four_end + 2 * f_strips * rows_e
    gathered = gathered.reshape(size, 2, -1, strip)
    one_rows, three_rows = f_strips * rows_e, f_strips * rows_h

    def block(chips, cores, rows):
        return (chips, cores, rows, strip)

    if rows_h % 16 == 0 and four_end % one_rows == 0 and one_end % three_rows == 0:
        one_at, three_at = four_end // one_rows, one_end // three_rows
        order = [b * group + j for j in range(group) for b in range(buckets)]
        weights = [
            (gathered, block(size, 2, one_rows), lambda m, c: (0, 0, one_at + c[0], 0)),
            (gathered, block(size, 1, four_end), lambda m, c: (0, c[0], 0, 0)),
            (gathered, block(size, 1, three_rows), lambda m, c: (0, c[0], three_at + c[0], 0)),
            (gathered, block(size, 1, three_rows), lambda m, c: (0, 1 - c[0], three_at + c[0], 0)),
        ]
    else:
        order = [0]
        four_half = gathered[:, :, :four_end].reshape(size, 2, e_strips, rows_f, strip)
        four_half = lax.dynamic_index_in_dim(four_half, core, 1, keepdims=False).swapaxes(0, 1)
        one_half = gathered[:, :, four_end:one_end].reshape(2 * size, 2, f_strips, rows_e, strip)
        one_half = lax.dynamic_index_in_dim(one_half, core, 1, keepdims=False).swapaxes(0, 1)
        three_half = gathered[:, :, one_end:].reshape(
            buckets, group, 2, 2, f_strips, rows_h, strip
        )
        three_half = lax.dynamic_index_in_dim(three_half, core, 3, keepdims=False)
        three_half = jnp.transpose(three_half, (2, 3, 1, 0, 4, 5))
        three_half = mine_other(three_half, 0)
        weights = [
            (x.reshape(1, 1, -1, strip), block(1, 1, x.size // strip), lambda m, c: (0, 0, 0, 0))
            for x in (one_half, four_half, *three_half)
        ]

    params = gather_bits(
        jnp.concatenate(
            [log_rate, ssm_coeff, jnp.broadcast_to(ssm_skip[:, None], (rows_h, 128))], axis=1
        ),
        size,
        sorted(top),
        top,
    ).reshape(chans, 1, -1)
    mix_params = (
        params[..., :nstate],
        params[..., nstate : 2 * nstate],
        params[..., 2 * nstate :],
    )
    tables = mixer_tables(*mix_params[:2])
    groups = [[b * group + j for j in range(group)] for b in range(buckets)]

    def exchange(x):
        return lax.all_to_all(x, "dp", split_axis=0, concat_axis=0, axis_index_groups=groups)

    def to_owner(x):
        return exchange(x.reshape(group, chans, tok_chip))

    def from_owner(x):
        return exchange(x).reshape(h_half, tok_chip)

    def swap_turned(x):
        got = swap_cores(x)
        return jnp.concatenate([got[:, tok_dev:], got[:, :tok_dev]], axis=1)

    device = 2 * chip + core
    lane = jnp.arange(tok_dev, dtype=jnp.int32)
    place = jnp.concatenate([device * tok_dev + lane, (device ^ 1) * tok_dev + lane])
    bucket_range = jnp.arange(buckets, dtype=jnp.int32)
    limit = jnp.sum(
        jnp.where((place // SEQ)[:, None] == bucket_range[None, :], lengths[None, :], 0), axis=1
    )
    live = (place % SEQ < limit).astype(F32)[:, None]

    normed, out_grad, reduced_t, two_slope, out_sum = norm_call(
        core_at,
        tok_pair,
        cot_pair,
        jnp.broadcast_to(live, (tok_chip, 128)),
        gain_f,
        nbias_f,
        two_turned,
        jnp.broadcast_to(btwo_f, (h_half, 128)),
    )
    v_seq = to_owner(reduced_t)
    y_seq, entering = mixer_forward(core_at, v_seq, tables, mix_params)
    y_own = from_owner(y_seq)
    y_other = swap_cores(y_own)

    def small_pack(grad_two, gain_sum, nbias_sum, out_sum, one_sum, gate_sum, two_sum):
        def by_device(x):
            return x.reshape(2 * size, -1)

        def by_core(x):
            zero = jnp.zeros_like(x)
            return by_device(natural_pair(x, zero, axis=1))

        grad_btwo = (
            jnp.sum(two_sum, axis=1).reshape(group, buckets, rows_h).swapaxes(0, 1).reshape(size, rows_h)
        )
        vec_grads = jnp.concatenate(
            [
                by_device(gain_sum),
                by_device(nbias_sum),
                by_device(out_sum),
                by_core(one_sum.reshape(size, rows_f)),
                by_core(gate_sum.reshape(size, rows_f)),
                by_core(grad_btwo),
            ],
            axis=1,
        )
        vec_grads = jnp.pad(vec_grads, ((0, 0), (0, vec_rows * h_half - vec_len)))
        return jnp.concatenate(
            [
                grad_two.reshape(2 * size, rows_e, h_half).astype(BF),
                vec_grads.reshape(2 * size, vec_rows, h_half).astype(BF),
            ],
            axis=1,
        )

    act_one, dz_slope, gate_grad, dy_mine, dy_other, gate_sum = early_call(
        core_at, normed, out_grad, bone_f, weights, order
    )
    dy_own = (dy_mine + swap_cores(dy_other).astype(F32)).astype(BF)
    dy_seq = to_owner(dy_own)

    back_a, back_b = order_a[::-1], order_b[::-1]

    def halve(x, have, bit):
        axis, mine = have.index(bit), bit_of(bit)
        theirs = lax.dynamic_index_in_dim(x, 1 - mine, axis, keepdims=False).astype(BF)
        kept = lax.dynamic_index_in_dim(x, mine, axis, keepdims=False)
        return kept, across(theirs, size, bit), [b for b in have if b != bit]

    def join(kept, got, *others):
        return kept.astype(F32) + after(got, *others).astype(F32)

    def begin(keep_send, have, bit, rest):
        have = [b for b in have if b != bit]
        keep, send = (x.reshape((2,) * len(have) + rest) for x in keep_send)
        return keep, across(send, size, bit), have

    def bit_at(bit):
        return jnp.reshape(bit_of(bit), (1,)).astype(jnp.int32)

    product, one_grad, out_mine, out_other, one_back, one_sum = late_call(
        core_at, after(y_own, dy_own), y_other, bthree_f, act_one, dz_slope, width, weights, order
    )
    out_got = swap_cores(out_other)
    grad_four = grad_call(
        bit_at(back_a[0]), after(product, dy_seq), out_grad, rows_f << back_a[0], 384, "grad_four"
    )
    four = begin(grad_four, natural, back_a[0], (rows_f, width))

    dv_seq, grad_rate, grad_coeff, grad_skip = mixer_backward(
        core_at, v_seq, after(dy_seq, grad_four[0]), entering, tables, mix_params
    )
    dv_own = from_owner(dv_seq)
    grad_one = grad_call(
        bit_at(back_b[0]), normed, after(one_grad, dv_seq), 2 * rows_e << back_b[0], 256, "grad_one"
    )
    one = begin(grad_one, natural, back_b[0], (2 * rows_e, f_half))
    grad_three = mixed_grad_call(
        bit_at(back_a[0]),
        y_own,
        y_other,
        after(gate_grad, grad_one[0]),
        buckets * rows_h << back_a[0],
        "grad_three",
    )
    three_bits = [bits] + by_owner
    three = begin(grad_three, three_bits, back_a[0], (rows_h, f_half))
    four = halve(join(four[0], four[1], grad_three[0]), four[2], back_a[1])

    two_grad_t, back_mine, back_other, gain_sum, nbias_sum, two_sum = tail_call(
        core_at,         after(dv_own, four[0]), two_slope, two_turned, one_back, tok_pair
    )
    grad_two = mm(normed, two_grad_t, 0, 1)
    mix_grads = jnp.concatenate([grad_rate[:, 0], grad_coeff[:, 0], grad_skip[:, 0]], axis=1)
    mix_grads = scatter_bits(
        mix_grads.reshape((2,) * len(top) + (rows_h, -1)), size, sorted(top)[::-1], top, F32
    )
    back_got = swap_cores(back_other)
    small_grads = small_pack(
        grad_two, gain_sum, nbias_sum, out_sum, one_sum, gate_sum, two_sum
    )
    small_got = lax.all_to_all(small_grads, everyone, split_axis=0, concat_axis=0)
    branch = out_mine + after(out_got, two_grad_t).astype(F32)
    mixed = (live[:tok_dev] * (tokens.astype(F32) + branch + bfour_f)).astype(BF)
    input_grad = input_call(core_at, back_mine, back_got, tokens, out_grad[:tok_dev], gain_f)

    def merge_f(mine, other):
        rows = mine.shape[0]
        parts = (mine.reshape(rows, size, rows_f), other.reshape(rows, size, rows_f))
        return natural_pair(*parts, axis=2).reshape(rows, 2 * f_half)

    def finish(state, order):
        kept, got, have = state
        for bit in order:
            kept, got, have = halve(join(kept, got, two_grad_t), have, bit)
        return join(kept, got, two_grad_t)

    sum_four = finish(four, back_a[2:])
    sum_one = finish(one, back_b[1:])
    one_keep, one_send = mine_other(sum_one.reshape(2, rows_e, f_half), 0)
    sum_one = merge_f(one_keep, swap_cores(one_send))
    sum_three = finish(three, back_a[1:])
    sum_three = merge_f(sum_three[0], swap_cores(sum_three[1]))

    small_sum = jnp.sum(
        small_got.reshape(size, 2, rows_e + vec_rows, h_half).astype(F32), axis=0
    )
    sum_two = jnp.transpose(
        small_sum[:, :rows_e].reshape(2, rows_e, group, buckets, rows_h), (1, 3, 2, 0, 4)
    ).reshape(rows_e, 2 * h_half)
    vec_sum = jnp.sum(small_sum[:, rows_e:], axis=0).reshape(-1)
    ends = [rows_e, 2 * rows_e, 3 * rows_e, 3 * rows_e + rows_f, 3 * rows_e + 2 * rows_f, vec_len]
    sum_gain, sum_nbias, sum_bfour, sum_bone, sum_bthree, sum_btwo = (
        vec_sum[a:b] for a, b in zip([0] + ends, ends)
    )

    return (
        mixed,
        input_grad,
        sum_gain,
        sum_nbias,
        sum_one,
        sum_bone,
        sum_two,
        sum_btwo,
        sum_three,
        sum_bthree,
        sum_four,
        sum_bfour,
        mix_grads[:, :nstate],
        mix_grads[:, nstate : 2 * nstate],
        mix_grads[:, 2 * nstate],
    )


def solution(mesh):
    both = ("dp", "fsdp")
    rows, vector = P(both, None), P(both)
    in_specs = (
        rows, rows, P(), vector, vector, rows, vector, rows, vector, rows, vector, rows, vector,
        rows, rows, vector,
    )
    out_specs = (
        rows, rows, vector, vector, rows, vector, rows, vector, rows, vector, rows, vector,
        rows, rows, vector,
    )
    return jax.shard_map(
        functools.partial(per_device, mesh.shape["dp"]),
        mesh=mesh,
        in_specs=in_specs,
        out_specs=out_specs,
        check_vma=False,
    )
```

time: 1320 us -> 448 us (0.34); the launches traced: 1300 us -> 444 us
  waiting for transfers between devices: 411 us -> 105 us
  matrix products: 224 us -> 3.81 us
  local copies, waits for them, and re-layouts: 315 us -> 98.8 us
  other arithmetic: 203 us -> 26.7 us
  Pallas kernels: 0 us -> 133 us
  blocking collectives: 112 us -> 0 us
  starting transfers between devices: 13.5 us -> 61.7 us
    reduce_scatter x4 -> x0, waiting for transfers between devices: 350 us -> none  [the longest x1 162 us: per_device(): lax.psum_scatter(grad_wfour, ('dp', 'fsdp'), scatter_dimension=0, tiled=T...]
    dot_general x24 -> x1, matrix products: 224 us -> 3.81 us  [mm(): lax.dot_general(left, right, (((left_dim,), (right_dim,)), ((), ())), pre...]
    dynamic_update_slice x128 -> x0, local copies, waits for them, and re-layouts: 139 us -> none  [state_mix(): final_state, entering = lax.scan(advance, start, block_ends)]
    pallas_call x0 -> x11, Pallas kernels: none -> 133 us  [the longest x8 94.6 us: call(): pl.pallas_call(kernel, grid_spec=pltpu.PrefetchScalarGridSpec(num_scalar_...]
    rev x2 -> x0, local copies, waits for them, and re-layouts: 129 us -> none  [state_mix(): decay[:, :, ::-1]]
    unnamed x2 -> x0, blocking collectives: 82.5 us -> none
    ppermute x0 -> x22, waiting for transfers between devices: none -> 78.6 us  [the longest x14 75.3 us: across(): return lax.ppermute(x, 'dp', [(i, i ^ 1 << bit) for i in range(size)])]
    broadcast_in_dim x64 -> x0, other arithmetic: 65.6 us -> none  [state_mix(): final_state, entering = lax.scan(advance, start, block_ends)]
  transfers between devices with their start and end apart: 11 -> 29, of which waited for: 6 -> 12; matrix products, arithmetic and copies ran while one was open for 34% -> 13% of each run, Pallas kernels for 0% -> 27%
where the time goes in v2:
time: 448 us; the launch traced here: 444 us
  Pallas kernels  133 us (30%)
  waiting for transfers between devices  105 us (23%)
  local copies, waits for them, and re-layouts  98.8 us (22%)
  starting transfers between devices  61.7 us (14%)
  other arithmetic  26.7 us (6%)
  between operations  15.6 us (3%)
    pallas_call x8, Pallas kernels, call(): pl.pallas_call(kernel, grid_spec=pltpu.PrefetchScalarGridSpec(num_scalar_...  94.6 us
    ppermute x14, waiting for transfers between devices, across(): return lax.ppermute(x, 'dp', [(i, i ^ 1 << bit) for i in range(size)])  75.3 us
    unnamed x136, local copies, waits for them, and re-layouts  67.6 us
    all_to_all x4, starting transfers between devices, exchange(): lax.all_to_all(x, 'dp', split_axis=0, concat_axis=0, axis_index_groups=gr...  32.2 us
    pallas_call x2, Pallas kernels, mixer_call(): pl.pallas_call(kernel, grid_spec=pltpu.PrefetchScalarGridSpec(num_scalar_...  28.8 us
    all_to_all x1, waiting for transfers between devices, per_device(): lax.all_to_all(small.reshape((2 * size,) + small.shape[2:]), everyone, sp...  26.4 us
    add x12, other arithmetic, join(): return kept.astype(F32) + after(got, *others).astype(F32)  14.3 us
    ppermute x14, starting transfers between devices, across(): return lax.ppermute(x, 'dp', [(i, i ^ 1 << bit) for i in range(size)])  14.3 us
  transfers between devices with their start and end apart: 29, of which 12 were waited for; matrix products, arithmetic and copies ran while one was open for 13% of the time, Pallas kernels for 27%

profile of v2, /device:TPU:0, one launch (start us, length us, event | category | flops | bytes accessed | tf_op | source)
XLA Modules:
  0.0 444.1 jit_solution(2945159046001865523)
XLA Ops:
  14.4 7.0 %all-to-all-start = ((bf16[32,34,256]{2,1,0:T(8,128)(2,1)}), bf16[32,34,256]{2,1,0:T(8,128)(2,1)S(1)}, u32[]{:S(2)}, u32[]{:S(2)}) async-start(bf16[32,34,256]{2,1,0:T(8,128)(2,1)} %bitcast.4), calls=%async_computation | async-start | bytes 1310720 | tf_op jit(solution)/shard_map/all_to_all | solution.py:831
  23.3 26.4 %all-to-all-done = bf16[32,34,256]{2,1,0:T(8,128)(2,1)S(1)} async-done(((bf16[32,34,256]{2,1,0:T(8,128)(2,1)}), bf16[32,34,256]{2,1,0:T(8,128)(2,1)S(1)}, u32[]{:S(2)}, u32[]{:S(2)}) %all-to-all-start) | async-done | bytes 557088 | tf_op jit(solution)/shard_map/all_to_all | solution.py:831
  52.5 3.8 constant_dynamic-update-slice_fusion.tok_ref
  56.3 2.2 pad_maximum_fusion.cot_ref
  59.1 7.0 %norm.1 = (bf16[2048,1024]{1,0:T(8,128)(2,1)S(1)}, bf16[2048,1024]{1,0:T(8,128)(2,1)S(1)}, bf16[256,2048]{1,0:T(8,128)(2,1)S(1)}, bf16[256,2048]{1,0:T(8,128)(2,1)S(1)}, f32[1,1024]{1,0:T(1,128)S(1)}) custom-call(s32[1]{0:T(128)} %bitcast._.turn_ref, bf16[2048,1024]{1,0:T(8,128)(2,1)S(1)} %copy-done.5, bf16[2048,1024]{1,0:T(8,128)(2,1)S(1)} %pad_maximum_fusion.cot_ref, ...), custom_call_target="tpu_custom_call" | custom-call | tf_op jit(solution)/shard_map/norm/pallas_call | solution.py:309
  72.1 3.6 all-to-all-start.1
  77.0 17.4 %collective-permute-done.2 = f32[16,1152]{1,0:T(8,128)S(1)} collective-permute-done((f32[16,1152]{1,0:T(8,128)S(1)}, f32[16,1152]{1,0:T(8,128)S(1)}, u32[]{:S(2)}, u32[]{:S(2)}) %collective-permute-start.2) | collective-permute-done | bytes 73760 | tf_op jit(solution)/shard_map/ppermute | solution.py:735
  94.6 9.0 %mixer_tables.1 = (bf16[32,256,512]{2,1,0:T(8,128)(2,1)S(1)}, bf16[32,512,256]{2,1,0:T(8,128)(2,1)S(1)}, bf16[32,256,256]{2,1,0:T(8,128)(2,1)S(1)}) custom-call(f32[32,1,512]{2,1,0:T(1,128)S(1)} %get-tuple-element.232.lr_ref, f32[32,1,512]{2,1,0:T(1,128)S(1)} %get-tuple-element.231.co_ref), custom_call_target="tpu_custom_call" | custom-call | tf_op jit(solution)/shard_map/mixer_tables/pallas_call | solution.py:247
  103.7 3.3 copy-done
  107.0 3.2 copy-done.1
  112.2 2.7 copy-done.12
  114.9 10.5 %mixer_forward.1 = (bf16[8,32,2048]{2,1,0:T(8,128)(2,1)S(1)}, f32[32,64,512]{2,1,0:T(8,128)S(1)}) custom-call(s32[1]{0:T(128)} %bitcast._.turn_ref, bf16[8,32,2048]{2,1,0:T(8,128)(2,1)S(1)} %all-to-all-done.1.v_ref, bf16[32,256,512]{2,1,0:T(8,128)(2,1)} %copy-done, bf16[32,512,256]{2,1,0:T(8,128)(2,1)} %copy-done.1, bf16[32,256,256]{2,1,0:T(8,128)(2,1)S(1)} %copy-done.12, ...), custom_call_target="tpu_custom_call" | custom-call | tf_op jit(solution)/shard_map/mixer_forward/pallas_call | solution.py:268
  128.3 19.1 %all-to-all-start.2 = ((bf16[8,32,2048]{2,1,0:T(8,128)(2,1)}), bf16[8,32,2048]{2,1,0:T(8,128)(2,1)S(1)}, u32[]{:S(2)}, u32[]{:S(2)}) async-start(bf16[8,32,2048]{2,1,0:T(8,128)(2,1)} %copy-done.37), calls=%async_computation.2 | async-start | bytes 2097152 | tf_op jit(solution)/shard_map/all_to_all | solution.py:912
  149.9 2.2 copy-done.9
  152.1 27.1 %early.1 = (bf16[2048,1536]{1,0:T(8,128)(2,1)}, bf16[2048,1536]{1,0:T(8,128)(2,1)}, bf16[2048,1536]{1,0:T(8,128)(2,1)}, f32[256,2048]{1,0:T(8,128)S(1)}, bf16[25...) custom-call(s32[1]{0:T(128)} %bitcast._.turn_ref, bf16[2048,1024]{1,0:T(8,128)(2,1)S(1)} %copy-done.9, ...), custom_call_target="tpu_custom_call" | custom-call | tf_op jit(solution)/shard_map/early/pallas_call | solution.py:309
  179.2 2.7 collective-permute-done.3
  183.2 5.1 %all-to-all-start.3 = ((bf16[8,32,2048]{2,1,0:T(8,128)(2,1)}), bf16[8,32,2048]{2,1,0:T(8,128)(2,1)}, u32[]{:S(2)}, u32[]{:S(2)}) async-start(bf16[8,32,2048]{2,1,0:T(8,128)(2,1)} %bitcast.146), calls=%async_computation.3 | async-start | bytes 2097152 | tf_op jit(solution)/shard_map/all_to_all | solution.py:912
  188.5 3.1 slice.122.g_ref
  191.9 25.0 %late.1 = (bf16[2048,1536]{1,0:T(8,128)(2,1)}, bf16[2048,1536]{1,0:T(8,128)(2,1)}, f32[1024,1024]{1,0:T(8,128)S(1)}, bf16[1024,1024]{1,0:T(8,128)(2,1)S(1)}, bf1...) custom-call(s32[1]{0:T(128)} %bitcast._.turn_ref, bf16[256,2048]{1,0:T(8,128)(2,1)S(1)} %bitcast.128, ...), custom_call_target="tpu_custom_call" | custom-call | tf_op jit(solution)/shard_map/late/pallas_call | solution.py:309
  222.2 2.2 copy-done.4
  224.4 2.8 copy-done.19
  227.2 8.3 %grad_four.1 = (f32[768,1024]{1,0:T(8,128)S(1)}, bf16[768,1024]{1,0:T(8,128)(2,1)S(1)}) custom-call(s32[1]{0:T(128)} %bitcast.21.bit_ref, bf16[2048,1536]{1,0:T(8,128)(2,1)S(1)} %copy-done.19, bf16[2048,1024]{1,0:T(8,128)(2,1)S(1)} %copy-done.4), custom_call_target="tpu_custom_call" | custom-call | tf_op jit(solution)/shard_map/grad_four/pallas_call | solution.py:309
  241.1 2.2 copy-done.13
  244.5 2.2 copy-done.28
  246.7 18.4 %mixer_backward.1 = (bf16[8,32,2048]{2,1,0:T(8,128)(2,1)S(1)}, f32[32,1,512]{2,1,0:T(1,128)S(1)}, f32[32,1,512]{2,1,0:T(1,128)S(1)}, f32[32,1,128]{2,1,0:T(1,128)S(1)}) custom-call(s32[1]{0:T(128)} %bitcast._.turn_ref, bf16[8,32,2048]{2,1,0:T(8,128)(2,1)S(1)} %copy-done.15, bf16[8,32,2048]{2,1,0:T(8,128)(2,1)} %all-to-all-done.3.dy_ref, ...), custom_call_target="tpu_custom_call" | custom-call | tf_op jit(solution)/shard_map/mixer_backward/pallas_call | solution.py:268
  266.1 4.4 all-to-all-start.4
  270.7 2.2 copy-done.10
  272.9 2.8 copy-done.18
  275.7 8.9 %grad_one.1 = (f32[512,1536]{1,0:T(8,128)S(1)}, bf16[512,1536]{1,0:T(8,128)(2,1)}) custom-call(s32[1]{0:T(128)} %bitcast.25.bit_ref, bf16[2048,1024]{1,0:T(8,128)(2,1)S(1)} %copy-done.10, bf16[2048,1536]{1,0:T(8,128)(2,1)S(1)} %copy-done.18), custom_call_target="tpu_custom_call" | custom-call | tf_op jit(solution)/shard_map/grad_one/pallas_call | solution.py:309
  286.3 2.8 copy-done.17
  289.1 6.4 %grad_three.1 = (f32[256,1536]{1,0:T(8,128)S(1)}, bf16[256,1536]{1,0:T(8,128)(2,1)}) custom-call(s32[1]{0:T(128)} %bitcast.21.bit_ref, bf16[256,2048]{1,0:T(8,128)(2,1)S(1)} %bitcast.129, bf16[256,2048]{1,0:T(8,128)(2,1)} %collective-permute-done.4.yo_ref, bf16[2048,1536]{1,0:T(8,128)(2,1)S(1)} %copy-done.17), custom_call_target="tpu_custom_call" | custom-call | tf_op jit(solution)/shard_map/grad_three/pallas_call | solution.py:309
  299.9 2.2 copy_add_fusion
  304.6 2.2 copy-done.6
  306.8 2.2 copy-done.26
  310.2 6.5 %tail.1 = (bf16[256,2048]{1,0:T(8,128)(2,1)S(1)}, f32[1024,1024]{1,0:T(8,128)S(1)}, bf16[1024,1024]{1,0:T(8,128)(2,1)S(1)}, f32[1,1024]{1,0:T(1,128)S(1)}, f32[1...) custom-call(s32[1]{0:T(128)} %bitcast._.turn_ref, bf16[256,2048]{1,0:T(8,128)(2,1)} %bitcast.22.dv_ref, ...), custom_call_target="tpu_custom_call" | custom-call | tf_op jit(solution)/shard_map/tail/pallas_call | solution.py:309
  321.1 13.7 %collective-permute-done.8 = bf16[2,2,2,64,1536]{4,3,2,1,0:T(8,128)(2,1)} collective-permute-done((bf16[2,2,2,64,1536]{4,3,2,1,0:T(8,128)(2,1)}, bf16[2,2,2,64,1536]{4,3,2,1,0:T(8,128)(2,1)}, u32[]{:S(2)}, u32[]{:S(2)}) %collective-permute-start.8) | collective-permute-done | bytes 1572896 | tf_op jit(solution)/shard_map/ppermute | solution.py:735
  339.8 3.8 convolution_convert_fusion
  344.5 6.5 %all-to-all-start.5 = ((bf16[32,34,256]{2,1,0:T(8,128)(2,1)}), bf16[32,34,256]{2,1,0:T(8,128)(2,1)S(1)}, u32[]{:S(2)}, u32[]{:S(2)}) async-start(bf16[32,34,256]{2,1,0:T(8,128)(2,1)} %pad_maximum_fusion.1), calls=%async_computation.5 | async-start | bytes 1310720 | tf_op jit(solution)/shard_map/all_to_all | solution.py:1045
  351.5 5.2 %multiply_convert_fusion = bf16[1024,1024]{1,0:T(8,128)(2,1)} fusion(f32[1024,1024]{1,0:T(8,128)} %copy-done.24, bf16[1024,1024]{1,0:T(8,128)(2,1)} %collective-permute-done.5, bf16[1024,1024]{1,0:T(8,128)(2,1)S(1)} %copy-done.7, f32[1024]{0:T(1024)S(1)} %add.169, f32[1024]{0:T(1024)S(1)} %slice-done), kind=kLoop, calls=%fused_computation.1 | loop fusion | flops 7340032 | bytes 10493952 | tf_op jit(solution)/shard_map/convert_element_type | solution.py:1047
  356.7 6.8 %collective-permute-done.14 = bf16[2,2,2,16,1536]{4,3,2,1,0:T(8,128)(2,1)S(1)} collective-permute-done((bf16[2,2,2,16,1536]{4,3,2,1,0:T(8,128)(2,1)}, bf16[2,2,2,16,1536]{4,3,2,1,0:T(8,128)(2,1)S(1)}, u32[]{:S(2)}, u32[]{:S(2)}) %collective-permute-start.14) | collective-permute-done | bytes 393248 | tf_op jit(solution)/shard_map/ppermute | solution.py:735
  363.7 2.7 collective-permute-start.15
  367.8 9.5 %collective-permute-done.15 = bf16[2,2,16,1536]{3,2,1,0:T(8,128)(2,1)S(1)} collective-permute-done((bf16[2,2,16,1536]{3,2,1,0:T(8,128)(2,1)S(1)}, bf16[2,2,16,1536]{3,2,1,0:T(8,128)(2,1)S(1)}, u32[]{:S(2)}, u32[]{:S(2)}) %collective-permute-start.15) | collective-permute-done | bytes 196640 | tf_op jit(solution)/shard_map/ppermute | solution.py:735
  380.0 3.2 collective-permute-done.16
  383.4 3.0 bitcast_add_fusion
  389.8 18.4 %collective-permute-done.19 = bf16[2,96,1024]{2,1,0:T(8,128)(2,1)} collective-permute-done((bf16[2,96,1024]{2,1,0:T(8,128)(2,1)}, bf16[2,96,1024]{2,1,0:T(8,128)(2,1)}, u32[]{:S(2)}, u32[]{:S(2)}) %collective-permute-start.19) | collective-permute-done | bytes 393248 | tf_op jit(solution)/shard_map/ppermute | solution.py:735
  419.6 4.1 collective-permute-done.11
  429.2 2.2 copy-done.23
  431.4 5.4 %input_grad.1 = bf16[1024,1024]{1,0:T(8,128)(2,1)} custom-call(s32[1]{0:T(128)} %bitcast._.turn_ref, f32[1024,1024]{1,0:T(8,128)S(1)} %copy-done.23, bf16[1024,1024]{1,0:T(8,128)(2,1)} %collective-permute-done.7.got_ref, bf16[1024,1024]{1,0:T(8,128)(2,1)S(1)} %copy-done.7, bf16[1024,1024]{1,0:T(8,128)(2,1)S(1)} %copy-done.16, f32[1,1024]{1,0:T(1,128)S(1)} %reshape.471.gain_ref), custom_call_target="tpu_custom_call" | custom-call | tf_op jit(solution)/shard_map/input_grad/pallas_call | solution.py:309
  (287 shorter events, 87.1 us)
Async XLA Ops:
  7.3 140.4 %all-gather.3.cloned.1.call-start = ((), (), s32[]{:S(2)}) async-start(), calls=%async_computation.6 | async-start | bytes 16220160 | tf_op jit(solution)/shard_map/all_gather | solution.py:860
  10.0 11.7 %copy-start.56 = (s32[2]{0:T(128)S(1)}, s32[2]{0:T(128)}, u32[]{:S(2)}) copy-start(s32[2]{0:T(128)} %param.18) | copy-start | bytes 28
  12.2 40.2 %collective-permute-start = (bf16[1024,1024]{1,0:T(8,128)(2,1)S(1)}, bf16[1024,1024]{1,0:T(8,128)(2,1)}, u32[]{:S(2)}, u32[]{:S(2)}) collective-permute-start(bf16[1024,1024]{1,0:T(8,128)(2,1)S(1)} %copy-done.7), channel_id=1, source_target_pairs={{0,1},{1,0},{2,3},{3,2},{4,5},{5,4},{6,7},{7,6},{8,9},{9,8},{10,11... | collective-permute-start | bytes 6291464 | tf_op jit(solution)/shard_map/ppermute | solution.py:731
  14.4 35.3 %all-to-all-start = ((bf16[32,34,256]{2,1,0:T(8,128)(2,1)}), bf16[32,34,256]{2,1,0:T(8,128)(2,1)S(1)}, u32[]{:S(2)}, u32[]{:S(2)}) async-start(bf16[32,34,256]{2,1,0:T(8,128)(2,1)} %bitcast.4), calls=%async_computation | async-start | bytes 1310720 | tf_op jit(solution)/shard_map/all_to_all | solution.py:831
  21.3 34.9 %collective-permute-start.1 = (bf16[1024,1024]{1,0:T(8,128)(2,1)}, bf16[1024,1024]{1,0:T(8,128)(2,1)}, u32[]{:S(2)}, u32[]{:S(2)}) collective-permute-start(bf16[1024,1024]{1,0:T(8,128)(2,1)} %param.17), channel_id=1, source_target_pairs={{0,1},{1,0},{2,3},{3,2},{4,5},{5,4},{6,7},{7,6},{8,9},{9,8},{10,11... | collective-permute-start | bytes 6291464 | tf_op jit(solution)/shard_map/ppermute | solution.py:731
  23.3 165.0 %copy-start.54 = (f32[2048]{0:T(1024)}, f32[2048]{0:T(1024)S(1)}, u32[]{:S(2)}) copy-start(f32[2048]{0:T(1024)S(1)} %fusion.12) | copy-start | bytes 24580
  59.1 16.6 %copy-start.57 = (f32[16]{0:T(128)S(1)}, f32[16]{0:T(128)}, u32[]{:S(2)}) copy-start(f32[16]{0:T(128)} %param.31) | copy-start | bytes 196
  59.1 16.7 %copy-start.52 = (f32[16,512]{1,0:T(8,128)S(1)}, f32[16,512]{1,0:T(8,128)}, u32[]{:S(2)}) copy-start(f32[16,512]{1,0:T(8,128)} %param.30) | copy-start | bytes 98308
  59.1 16.7 %copy-start.53 = (f32[16,512]{1,0:T(8,128)S(1)}, f32[16,512]{1,0:T(8,128)}, u32[]{:S(2)}) copy-start(f32[16,512]{1,0:T(8,128)} %param.29) | copy-start | bytes 98308
  72.1 40.1 %all-to-all-start.1 = ((bf16[8,32,2048]{2,1,0:T(8,128)(2,1)}), bf16[8,32,2048]{2,1,0:T(8,128)(2,1)S(1)}, u32[]{:S(2)}, u32[]{:S(2)}) async-start(bf16[8,32,2048]{2,1,0:T(8,128)(2,1)} %bitcast.136), calls=%async_computation.1 | async-start | bytes 2097152 | tf_op jit(solution)/shard_map/all_to_all | solution.py:912
  75.8 18.6 %collective-permute-start.2 = (f32[16,1152]{1,0:T(8,128)S(1)}, f32[16,1152]{1,0:T(8,128)S(1)}, u32[]{:S(2)}, u32[]{:S(2)}) collective-permute-start(f32[16,1152]{1,0:T(8,128)S(1)} %pad_maximum_fusion.8), channel_id=1, source_target_pairs={{0,16},{2,18},{4,20},{6,22},{8,24},{10,26},{12,28},{14,30},{16,0},... | collective-permute-start | bytes 221192 | tf_op jit(solution)/shard_map/ppermute | solution.py:735
  112.2 13.1 %copy-start.14 = (bf16[8,32,2048]{2,1,0:T(8,128)(2,1)}, bf16[8,32,2048]{2,1,0:T(8,128)(2,1)S(1)}, u32[]{:S(2)}) copy-start(bf16[8,32,2048]{2,1,0:T(8,128)(2,1)S(1)} %all-to-all-done.1.v_ref) | copy-start | bytes 3145732
  128.3 54.8 %all-to-all-start.2 = ((bf16[8,32,2048]{2,1,0:T(8,128)(2,1)}), bf16[8,32,2048]{2,1,0:T(8,128)(2,1)S(1)}, u32[]{:S(2)}, u32[]{:S(2)}) async-start(bf16[8,32,2048]{2,1,0:T(8,128)(2,1)} %copy-done.37), calls=%async_computation.2 | async-start | bytes 2097152 | tf_op jit(solution)/shard_map/all_to_all | solution.py:912
  179.2 2.7 collective-permute-start.3
  183.2 39.0 %all-to-all-start.3 = ((bf16[8,32,2048]{2,1,0:T(8,128)(2,1)}), bf16[8,32,2048]{2,1,0:T(8,128)(2,1)}, u32[]{:S(2)}, u32[]{:S(2)}) async-start(bf16[8,32,2048]{2,1,0:T(8,128)(2,1)} %bitcast.146), calls=%async_computation.3 | async-start | bytes 2097152 | tf_op jit(solution)/shard_map/all_to_all | solution.py:912
  188.3 3.6 collective-permute-start.4
  238.6 61.3 %collective-permute-start.6 = (bf16[2,2,2,96,1024]{4,3,1,0,2:T(8,128)(2,1)}, bf16[2,2,2,96,1024]{4,3,1,0,2:T(8,128)(2,1)}, u32[]{:S(2)}, u32[]{:S(2)}) collective-permute-start(bf16[2,2,2,96,1024]{4,3,1,0,2:T(8,128)(2,1)} %copy.191), channel_id=1, source_target_pairs={{0,4},{2,6},{4,0},{6,2},{8,12},{10,14},{12,8},{14,10},{16,20},{18,... | collective-permute-start | bytes 4718600 | tf_op jit(solution)/shard_map/ppermute | solution.py:735
  240.8 110.6 %collective-permute-start.5 = (bf16[1024,1024]{1,0:T(8,128)(2,1)}, bf16[1024,1024]{1,0:T(8,128)(2,1)}, u32[]{:S(2)}, u32[]{:S(2)}) collective-permute-start(bf16[1024,1024]{1,0:T(8,128)(2,1)} %copy-done.41), channel_id=1, source_target_pairs={{0,1},{1,0},{2,3},{3,2},{4,5},{5,4},{6,7},{7,6},{8,9},{9,8},{10,11... | collective-permute-start | bytes 6291464 | tf_op jit(solution)/shard_map/ppermute | solution.py:731
  266.1 38.5 %all-to-all-start.4 = ((bf16[8,32,2048]{2,1,0:T(8,128)(2,1)}), bf16[8,32,2048]{2,1,0:T(8,128)(2,1)}, u32[]{:S(2)}, u32[]{:S(2)}) async-start(bf16[8,32,2048]{2,1,0:T(8,128)(2,1)} %copy-done.35), calls=%async_computation.4 | async-start | bytes 2097152 | tf_op jit(solution)/shard_map/all_to_all | solution.py:912
  270.6 28.0 %collective-permute-start.21 = (f32[16,1152]{1,0:T(8,128)S(1)}, f32[16,1152]{1,0:T(8,128)S(1)}, u32[]{:S(2)}, u32[]{:S(2)}) collective-permute-start(f32[16,1152]{1,0:T(8,128)S(1)} %dynamic-slice_bitcast_fusion.1), channel_id=1, source_target_pairs={{0,16},{2,18},{4,20},{6,22},{8,24},{10,26},{12,28},{14,30},{16,0},... | collective-permute-start | bytes 221192 | tf_op jit(solution)/shard_map/ppermute | solution.py:735
  289.1 10.8 %copy-start.30 = (f32[768,1024]{1,0:T(8,128)S(1)}, f32[768,1024]{1,0:T(8,128)}, u32[]{:S(2)}) copy-start(f32[768,1024]{1,0:T(8,128)} %copy-done.29) | copy-start | bytes 9437188
  295.5 6.6 %copy-start.33 = (f32[256,1536]{1,0:T(8,128)}, f32[256,1536]{1,0:T(8,128)S(1)}, u32[]{:S(2)}) copy-start(f32[256,1536]{1,0:T(8,128)S(1)} %get-tuple-element.98) | copy-start | bytes 4718596
  295.5 21.2 %collective-permute-start.13 = (bf16[2,2,2,2,16,1536]{5,4,3,2,1,0:T(8,128)(2,1)}, bf16[2,2,2,2,16,1536]{5,4,3,2,1,0:T(8,128)(2,1)}, u32[]{:S(2)}, u32[]{:S(2)}) collective-permute-start(bf16[2,2,2,2,16,1536]{5,4,3,2,1,0:T(8,128)(2,1)} %bitcast.50), channel_id=1, source_target_pairs={{0,4},{2,6},{4,0},{6,2},{8,12},{10,14},{12,8},{14,10},{16,20},{18,... | collective-permute-start | bytes 2359304 | tf_op jit(solution)/shard_map/ppermute | solution.py:735
  297.2 37.6 %collective-permute-start.8 = (bf16[2,2,2,64,1536]{4,3,2,1,0:T(8,128)(2,1)}, bf16[2,2,2,64,1536]{4,3,2,1,0:T(8,128)(2,1)}, u32[]{:S(2)}, u32[]{:S(2)}) collective-permute-start(bf16[2,2,2,64,1536]{4,3,2,1,0:T(8,128)(2,1)} %bitcast.37), channel_id=1, source_target_pairs={{0,2},{2,0},{4,6},{6,4},{8,10},{10,8},{12,14},{14,12},{16,18},{18,... | collective-permute-start | bytes 4718600 | tf_op jit(solution)/shard_map/ppermute | solution.py:735
  304.0 62.4 %collective-permute-start.18 = (bf16[2,2,96,1024]{3,2,1,0:T(8,128)(2,1)}, bf16[2,2,96,1024]{3,2,1,0:T(8,128)(2,1)}, u32[]{:S(2)}, u32[]{:S(2)}) collective-permute-start(bf16[2,2,96,1024]{3,2,1,0:T(8,128)(2,1)} %fusion.1), channel_id=1, source_target_pairs={{0,2},{2,0},{4,6},{6,4},{8,10},{10,8},{12,14},{14,12},{16,18},{18,... | collective-permute-start | bytes 2359304 | tf_op jit(solution)/shard_map/ppermute | solution.py:735
  310.2 6.6 %copy-start.34 = (f32[256,1536]{1,0:T(8,128)S(1)}, f32[256,1536]{1,0:T(8,128)}, u32[]{:S(2)}) copy-start(f32[256,1536]{1,0:T(8,128)} %copy-done.33) | copy-start | bytes 4718596
  316.7 20.1 %copy-start.22 = (f32[1024,1024]{1,0:T(8,128)}, f32[1024,1024]{1,0:T(8,128)S(1)}, u32[]{:S(2)}) copy-start(f32[1024,1024]{1,0:T(8,128)S(1)} %get-tuple-element.105.mine_ref) | copy-start | bytes 12582916
  316.7 20.1 %copy-start.40 = (bf16[1024,1024]{1,0:T(8,128)(2,1)}, bf16[1024,1024]{1,0:T(8,128)(2,1)S(1)}, u32[]{:S(2)}) copy-start(bf16[1024,1024]{1,0:T(8,128)(2,1)S(1)} %get-tuple-element.106) | copy-start | bytes 6291460
  316.7 20.1 %copy-start.42 = (bf16[256,2048]{1,0:T(8,128)(2,1)}, bf16[256,2048]{1,0:T(8,128)(2,1)S(1)}, u32[]{:S(2)}) copy-start(bf16[256,2048]{1,0:T(8,128)(2,1)S(1)} %get-tuple-element.103) | copy-start | bytes 3145732
  316.7 18.1 %copy-start.32 = (f32[512,1536]{1,0:T(8,128)S(1)}, f32[512,1536]{1,0:T(8,128)}, u32[]{:S(2)}) copy-start(f32[512,1536]{1,0:T(8,128)} %copy-done.31) | copy-start | bytes 9437188
  318.9 17.9 %copy-start.46 = (f32[2,2,2,2,16,1536]{5,4,3,2,1,0:T(8,128)}, f32[2,2,2,2,16,1536]{5,4,3,2,1,0:T(8,128)S(1)}, u32[]{:S(2)}) copy-start(f32[2,2,2,2,16,1536]{5,4,3,2,1,0:T(8,128)S(1)} %convert_add_fusion.2) | copy-start | bytes 4718596
  319.7 43.8 %collective-permute-start.14 = (bf16[2,2,2,16,1536]{4,3,2,1,0:T(8,128)(2,1)}, bf16[2,2,2,16,1536]{4,3,2,1,0:T(8,128)(2,1)S(1)}, u32[]{:S(2)}, u32[]{:S(2)}) collective-permute-start(bf16[2,2,2,16,1536]{4,3,2,1,0:T(8,128)(2,1)} %fusion.3), channel_id=1, source_target_pairs={{0,2},{2,0},{4,6},{6,4},{8,10},{10,8},{12,14},{14,12},{16,18},{18,... | collective-permute-start | bytes 1179656 | tf_op jit(solution)/shard_map/ppermute | solution.py:735
  338.8 44.7 %collective-permute-start.9 = (bf16[2,2,64,1536]{3,2,1,0:T(8,128)(2,1)}, bf16[2,2,64,1536]{3,2,1,0:T(8,128)(2,1)}, u32[]{:S(2)}, u32[]{:S(2)}) collective-permute-start(bf16[2,2,64,1536]{3,2,1,0:T(8,128)(2,1)} %fusion), channel_id=1, source_target_pairs={{0,4},{2,6},{4,0},{6,2},{8,12},{10,14},{12,8},{14,10},{16,20},{18,... | collective-permute-start | bytes 2359304 | tf_op jit(solution)/shard_map/ppermute | solution.py:735
  339.8 11.7 %slice-start = ((f32[2048]{0:T(1024)}), f32[1024]{0:T(1024)S(1)}, s32[]{:S(2)}) async-start(f32[2048]{0:T(1024)} %copy-done.54), calls=%async_computation.7 | async-start | bytes 8192 | tf_op jit(solution)/shard_map/slice | solution.py:1047
  344.5 66.1 %all-to-all-start.5 = ((bf16[32,34,256]{2,1,0:T(8,128)(2,1)}), bf16[32,34,256]{2,1,0:T(8,128)(2,1)S(1)}, u32[]{:S(2)}, u32[]{:S(2)}) async-start(bf16[32,34,256]{2,1,0:T(8,128)(2,1)} %pad_maximum_fusion.1), calls=%async_computation.5 | async-start | bytes 1310720 | tf_op jit(solution)/shard_map/all_to_all | solution.py:1045
  351.0 76.6 %collective-permute-start.7 = (bf16[1024,1024]{1,0:T(8,128)(2,1)}, bf16[1024,1024]{1,0:T(8,128)(2,1)}, u32[]{:S(2)}, u32[]{:S(2)}) collective-permute-start(bf16[1024,1024]{1,0:T(8,128)(2,1)} %copy-done.40), channel_id=1, source_target_pairs={{0,1},{1,0},{2,3},{3,2},{4,5},{5,4},{6,7},{7,6},{8,9},{9,8},{10,11... | collective-permute-start | bytes 6291464 | tf_op jit(solution)/shard_map/ppermute | solution.py:731
  351.4 12.1 %copy-start.47 = (f32[2,2,2,2,16,1536]{5,4,3,2,1,0:T(8,128)S(1)}, f32[2,2,2,2,16,1536]{5,4,3,2,1,0:T(8,128)}, u32[]{:S(2)}) copy-start(f32[2,2,2,2,16,1536]{5,4,3,2,1,0:T(8,128)} %copy-done.46) | copy-start | bytes 4718596
  351.4 14.9 %copy-start.44 = (f32[2,2,2,96,1024]{4,3,1,0,2:T(8,128)S(1)}, f32[2,2,2,96,1024]{4,3,1,0,2:T(8,128)}, u32[]{:S(2)}) copy-start(f32[2,2,2,96,1024]{4,3,1,0,2:T(8,128)} %copy-done.43) | copy-start | bytes 9437188
  363.7 13.6 %collective-permute-start.15 = (bf16[2,2,16,1536]{3,2,1,0:T(8,128)(2,1)S(1)}, bf16[2,2,16,1536]{3,2,1,0:T(8,128)(2,1)S(1)}, u32[]{:S(2)}, u32[]{:S(2)}) collective-permute-start(bf16[2,2,16,1536]{3,2,1,0:T(8,128)(2,1)S(1)} %fusion.6), channel_id=1, source_target_pairs={{0,16},{2,18},{4,20},{6,22},{8,24},{10,26},{12,28},{14,30},{16,0},... | collective-permute-start | bytes 589832 | tf_op jit(solution)/shard_map/ppermute | solution.py:735
  367.7 9.6 %copy-start.48 = (f32[2,2,96,1024]{3,2,1,0:T(8,128)}, f32[2,2,96,1024]{3,2,1,0:T(8,128)S(1)}, u32[]{:S(2)}) copy-start(f32[2,2,96,1024]{3,2,1,0:T(8,128)S(1)} %convert_add_fusion.1) | copy-start | bytes 4718596
  377.3 5.9 %collective-permute-start.16 = (bf16[2,16,1536]{2,1,0:T(8,128)(2,1)S(1)}, bf16[2,16,1536]{2,1,0:T(8,128)(2,1)S(1)}, u32[]{:S(2)}, u32[]{:S(2)}) collective-permute-start(bf16[2,16,1536]{2,1,0:T(8,128)(2,1)S(1)} %fusion.8), channel_id=1, source_target_pairs={{0,8},{2,10},{4,12},{6,14},{8,0},{10,2},{12,4},{14,6},{16,24},{18,... | collective-permute-start | bytes 294920 | tf_op jit(solution)/shard_map/ppermute | solution.py:735
  378.2 30.0 %collective-permute-start.19 = (bf16[2,96,1024]{2,1,0:T(8,128)(2,1)}, bf16[2,96,1024]{2,1,0:T(8,128)(2,1)}, u32[]{:S(2)}, u32[]{:S(2)}) collective-permute-start(bf16[2,96,1024]{2,1,0:T(8,128)(2,1)} %fusion.4), channel_id=1, source_target_pairs={{0,16},{2,18},{4,20},{6,22},{8,24},{10,26},{12,28},{14,30},{16,0},... | collective-permute-start | bytes 1179656 | tf_op jit(solution)/shard_map/ppermute | solution.py:735
  383.2 3.2 collective-permute-start.17
  389.8 25.7 %collective-permute-start.10 = (bf16[2,64,1536]{2,1,0:T(8,128)(2,1)}, bf16[2,64,1536]{2,1,0:T(8,128)(2,1)}, u32[]{:S(2)}, u32[]{:S(2)}) collective-permute-start(bf16[2,64,1536]{2,1,0:T(8,128)(2,1)} %fusion.2), channel_id=1, source_target_pairs={{0,16},{2,18},{4,20},{6,22},{8,24},{10,26},{12,28},{14,30},{16,0},... | collective-permute-start | bytes 1179656 | tf_op jit(solution)/shard_map/ppermute | solution.py:735
  410.6 9.0 %collective-permute-start.20 = (bf16[96,1024]{1,0:T(8,128)(2,1)}, bf16[96,1024]{1,0:T(8,128)(2,1)S(1)}, u32[]{:S(2)}, u32[]{:S(2)}) collective-permute-start(bf16[96,1024]{1,0:T(8,128)(2,1)} %fusion.7), channel_id=1, source_target_pairs={{0,8},{2,10},{4,12},{6,14},{8,0},{10,2},{12,4},{14,6},{16,24},{18,... | collective-permute-start | bytes 589832 | tf_op jit(solution)/shard_map/ppermute | solution.py:735
  410.7 13.2 %copy-start.50 = (f32[2,96,1024]{2,1,0:T(8,128)S(1)}, f32[2,96,1024]{2,1,0:T(8,128)}, u32[]{:S(2)}) copy-start(f32[2,96,1024]{2,1,0:T(8,128)} %copy-done.49) | copy-start | bytes 2359300
  416.9 6.8 %collective-permute-start.11 = (bf16[64,1536]{1,0:T(8,128)(2,1)S(1)}, bf16[64,1536]{1,0:T(8,128)(2,1)S(1)}, u32[]{:S(2)}, u32[]{:S(2)}) collective-permute-start(bf16[64,1536]{1,0:T(8,128)(2,1)S(1)} %fusion.5), channel_id=1, source_target_pairs={{0,8},{2,10},{4,12},{6,14},{8,0},{10,2},{12,4},{14,6},{16,24},{18,... | collective-permute-start | bytes 589832 | tf_op jit(solution)/shard_map/ppermute | solution.py:735
  423.8 1.5 collective-permute-start.12
  (46 other events, 129.6 us)
Sparse Core Ops, SparseCore 0:
  12.4 127.6 all-gather.2
